TPU v7x, 32 devices: a whole 2x2x4 slice. The times are simulated.
32 devices in a mesh: segment: 8 (over z, y), seq: 4 (over x, core).
Axes of the slice: x: 2, y: 2, z: 4, core: 2. Of those that a mesh axis runs over, the one named last changes fastest.
Arguments:
- queue: bfloat16 [8, 512, 3072], P('segment', 'seq'), may hold values from -4 to 4
- fresh_noise: bfloat16 [512, 3072], P('seq'), may hold values from -6 to 6
- w_mod: bfloat16 [8, 3072, 9216], P('segment', None, 'seq'), may hold values from -0.109375 to 0.109375
- w_qkv: bfloat16 [8, 3072, 4, 384], P('segment', None, 'seq'), may hold values from -0.109375 to 0.109375
- w_out: bfloat16 [8, 512, 3072], P('segment', 'seq'), may hold values from -0.25 to 0.25
- q_gain: float32 [8, 128], P('segment'), may hold values from 1.5 to 7, as said below
- k_gain: float32 [8, 128], P('segment'), may hold values from 1.5 to 7, as said below
- levels: int32 [8], P('segment'), may hold values from 0 to 49
- plan: int32 [50], replicated, may hold values from 0 to 999
- positions: int32 [8], P('segment'), may hold values from 0 to 1023
Outputs:
- queue_next: bfloat16 [8, 512, 3072], P('segment', 'seq')
- clean_frame: bfloat16 [512, 3072], P('seq', 'segment')
Inputs may be any that keep to these rules, and one draw needn't show every extreme that they name: `q_gain`: query gains are positive. `k_gain`: key gains are positive.
All inputs are finite; a program needn't handle non-finite values.
Results may differ from a plain program's by a relative error of at most 0.035.
Values may be sent and summed in bfloat16 or wider, within the bound.
A program may use at most 128 MiB of HBM per device.

v0:
```python
import math

import jax
import jax.numpy as jnp
from jax import lax
from jax.sharding import PartitionSpec as P

GRID_W = 32


EPSILON = 1e-06
ROPE_BASE = 256.0


def with_halo(cells, sides, width):
    for axis, dim in sides:
        count = lax.axis_size(axis)
        ends = count - 1
        head = lax.slice_in_dim(cells, 0, width, axis=dim)
        tail = lax.slice_in_dim(cells, cells.shape[dim] - width, cells.shape[dim], axis=dim)
        cells = jnp.concatenate(
            [
                lax.ppermute(tail, axis, [(i, (i + 1) % count) for i in range(ends)]),
                cells,
                lax.ppermute(head, axis, [((i + 1) % count, i) for i in range(ends)]),
            ],
            axis=dim,
        )
    return cells


def passed_along(value, axis, by):
    length = lax.axis_size(axis)
    pairs = [(i, i + by) for i in range(length) if 0 <= i + by < length]
    return lax.ppermute(value, axis, pairs)


def broadcast(value, axis, root):
    mine = lax.axis_index(axis) == root
    return lax.psum(jnp.where(mine, value, jnp.zeros_like(value)), axis)


def time_embedding(step_values, width):
    half_width = width // 2
    counter = jnp.arange(half_width, dtype=jnp.float32)
    frequency = jnp.exp(-jnp.log(10000.0) * counter / half_width)
    angles = step_values.astype(jnp.float32)[:, None] * frequency[None, :]
    return jnp.concatenate([jnp.cos(angles), jnp.sin(angles)], axis=-1)


def rope_angles(frame_position, row_count, head_dim, grid_width):
    time_dim = head_dim // 8
    space_dim = (head_dim - time_dim) // 2
    tokens_at = jnp.arange(row_count, dtype=jnp.int32)
    grid_row = (tokens_at // grid_width).astype(jnp.float32)
    grid_col = (tokens_at % grid_width).astype(jnp.float32)
    moment = jnp.zeros((row_count,), jnp.float32) + frame_position.astype(jnp.float32)
    sections = []
    for coords, section in ((moment, time_dim), (grid_row, space_dim), (grid_col, space_dim)):
        half_size = section // 2
        frequency = ROPE_BASE ** (-2.0 * jnp.arange(half_size, dtype=jnp.float32) / section)
        angles = coords[:, None] * frequency[None, :]
        sections.append(jnp.concatenate([angles, angles], axis=-1))
    return jnp.concatenate(sections, axis=-1)


def rotate_half(values, head_dim):
    time_dim = head_dim // 8
    space_dim = (head_dim - time_dim) // 2
    pieces_out = []
    position = 0
    for section in (time_dim, space_dim, space_dim):
        half_size = section // 2
        leading = values[..., position : position + half_size]
        second = values[..., position + half_size : position + section]
        pieces_out.append(jnp.concatenate([-second, leading], axis=-1))
        position += section
    return jnp.concatenate(pieces_out, axis=-1)


def apply_rope(values, angles, head_dim):
    return values * jnp.cos(angles) + rotate_half(values, head_dim) * jnp.sin(angles)


def rms_gain(values, gains):
    mean_square = jnp.mean(values * values, axis=-1, keepdims=True)
    return values * lax.rsqrt(mean_square + EPSILON) * gains


def layer_norm(values):
    centre = jnp.mean(values, axis=-1, keepdims=True)
    spread = jnp.mean(jnp.square(values - centre), axis=-1, keepdims=True)
    return (values - centre) * lax.rsqrt(spread + EPSILON)


def attend(query_rows, key_rows, value_rows, usable, head_dim):
    scores = jnp.dot(query_rows, key_rows.T, preferred_element_type=jnp.float32) * head_dim ** (
        -0.5
    )
    scores = jnp.where(usable[None, :], scores, -jnp.inf)
    row_max = jnp.max(scores, axis=-1, keepdims=True)
    raised = jnp.exp(scores - row_max)
    weights = (raised / jnp.sum(raised, axis=-1, keepdims=True)).astype(jnp.bfloat16)
    return jnp.dot(weights, value_rows, preferred_element_type=jnp.float32).astype(jnp.bfloat16)


def shards(queue, fresh_noise, w_mod, w_qkv, w_out, q_gain, k_gain, levels, plan, positions):
    segments = lax.axis_size("segment")
    seq_count = lax.axis_size("seq")
    segment_at = lax.axis_index("segment")
    tok_dev = queue.shape[1]
    width = queue.shape[2]
    heads_here = w_qkv.shape[2]
    head_dim = w_qkv.shape[3] // 3
    tok_frame = tok_dev * seq_count
    picked = levels[:, None] == jnp.arange(plan.shape[0], dtype=jnp.int32)[None, :]
    step_values = jnp.sum(jnp.where(picked, plan[None, :], 0), axis=1)
    embedding = jax.nn.silu(time_embedding(step_values, width)).astype(jnp.bfloat16)
    mod_part = jnp.dot(embedding, w_mod[0], preferred_element_type=jnp.float32)
    modulation = lax.all_gather(mod_part, "seq", axis=1, tiled=True)[0]
    shift_row = modulation[:width]
    scale_row = modulation[width : 2 * width]
    gate_row = modulation[2 * width :]
    resident = queue[0].astype(jnp.float32)
    modulated = (layer_norm(resident) * (1.0 + scale_row) + shift_row).astype(jnp.bfloat16)
    flat_weight = w_qkv[0].reshape(width, heads_here * 3 * head_dim)
    projected_qkv = jnp.dot(
        lax.all_gather(modulated, "seq", axis=0, tiled=True),
        flat_weight,
        preferred_element_type=jnp.float32,
    )
    projected_qkv = projected_qkv.reshape(tok_frame, heads_here, 3 * head_dim)
    angles = rope_angles(positions[0], tok_frame, head_dim, GRID_W)[:, None, :]
    queries = apply_rope(
        rms_gain(projected_qkv[..., :head_dim], q_gain[0]), angles, head_dim
    ).astype(jnp.bfloat16)
    key_rows = apply_rope(
        rms_gain(projected_qkv[..., head_dim : 2 * head_dim], k_gain[0]), angles, head_dim
    ).astype(jnp.bfloat16)
    value_rows = projected_qkv[..., 2 * head_dim :].astype(jnp.bfloat16)
    stacked = jnp.stack([key_rows, value_rows])[None]
    beside_all = with_halo(stacked, (("segment", 0),), 1)
    earlier = beside_all[0]
    following = beside_all[2]
    near_keys = jnp.concatenate([earlier[0], key_rows, following[0]], axis=0)
    near_values = jnp.concatenate([earlier[1], value_rows, following[1]], axis=0)
    filled = jnp.ones((tok_frame,), dtype=bool)
    usable = jnp.concatenate(
        [filled & (segment_at > 0), filled, filled & (segment_at < segments - 1)]
    )
    block_rows = math.gcd(tok_frame, 512)
    block_count = tok_frame // block_rows
    head_keys = near_keys[:, 0]
    head_values = near_values[:, 0]
    query_blocks = queries[:, 0].reshape(block_count, block_rows, head_dim)

    def one_block(query_rows, head_keys=head_keys, head_values=head_values):
        return attend(query_rows, head_keys, head_values, usable, head_dim)

    outputs = [lax.map(one_block, query_blocks).reshape(tok_frame, head_dim)]
    attended = jnp.stack(outputs, axis=1).reshape(tok_frame, heads_here * head_dim)
    projected = lax.psum_scatter(
        jnp.dot(attended, w_out[0], preferred_element_type=jnp.float32).astype(jnp.bfloat16),
        "seq",
        scatter_dimension=0,
        tiled=True,
    ).astype(jnp.float32)
    finished = (resident + gate_row * projected).astype(jnp.bfloat16)
    arrived = passed_along(finished, "segment", 1)
    queue_next = jnp.where(segment_at == 0, fresh_noise, arrived)[None]
    clean_whole = broadcast(finished, "segment", segments - 1)
    column_count = width // segments
    clean_frame = lax.dynamic_slice_in_dim(clean_whole, segment_at * column_count, column_count, 1)
    return (queue_next, clean_frame)


def solution(mesh):
    placed = (
        P("segment", "seq", None),
        P("seq", None),
        P("segment", None, "seq"),
        P("segment", None, "seq", None),
        P("segment", "seq", None),
        P("segment", None),
        P("segment", None),
        P("segment"),
        P(),
        P("segment"),
    )
    return jax.shard_map(
        shards,
        mesh=mesh,
        in_specs=placed,
        out_specs=(P("segment", "seq", None), P("seq", "segment")),
        check_vma=False,
    )
```

profile of v0, /device:TPU:8, one launch (start us, length us, event | category | flops | bytes accessed | tf_op | source)
XLA Modules:
  0.0 233.5 jit_solution(17650625161579900962)
XLA Ops:
  7.2 0.0 copy-start
  7.2 0.0 all-gather.4.cloned.1.call-start
  8.0 1.3 fusion.51
  10.0 0.1 fusion.40
  10.1 0.0 copy-start.2
  10.1 7.0 %fusion.3 = f32[1,1,2304]{2,1,0:T(1,128)S(1)} fusion(bf16[3072,1]{0,1:T(2,128)(2,1)S(1)} %reshape.623, bf16[1,3072,2304]{2,1,0:T(8,128)(2,1)} %param.12), kind=kOutput, calls=%fused_computation.5 | convolution fusion | flops 14155776 | bytes 14171136 | tf_op jit(solution)/shard_map/dot_general | solution.py:119
  17.1 5.2 %all-gather.1 = f32[4,1,2304]{2,1,0:T(1,128)S(1)} all-gather(f32[1,1,2304]{2,1,0:T(1,128)S(1)} %fusion.3), channel_id=2, replica_groups=mesh['segment'=8,'seq'=4] {'seq'}, dimensions={0}, use_global_device_ids=true | all-gather | bytes 46080 | tf_op jit(solution)/shard_map/all_gather | solution.py:120
  22.3 0.6 fusion.61
  22.9 0.0 copy-done.2
  22.9 0.2 convert_reduce_fusion
  23.1 0.4 fusion.13
  23.5 1.3 fusion.16
  24.8 0.0 all-gather.4.cloned.1.call-update
  24.8 0.0 reduce-scatter.2.cloned.1.call-start
  25.5 0.1 multiply_bitcast_fusion
  25.6 0.1 concatenate.73
  25.7 0.3 concatenate.76
  26.1 0.6 pad_add_fusion
  26.7 1.7 fusion.58
  28.3 26.4 %all-gather.4.cloned.1.call-done = bf16[512,3072]{1,0:T(8,128)(2,1)} async-done(((bf16[128,3072]{1,0:T(8,128)(2,1)}), bf16[512,3072]{1,0:T(8,128)(2,1)}) %all-gather.4.cloned.1.call-update) | async-done | bytes 3145744 | tf_op jit(solution)/shard_map/all_gather | solution.py:128
  54.7 0.0 copy-done
  54.7 3.3 %fusion.19 = f32[512,1,384]{0,2,1:T(8,128)S(1)} fusion(bf16[512,3072]{1,0:T(8,128)(2,1)} %all-gather.4.cloned.1.call-done, bf16[1,3072,1,384]{3,1,2,0:T(8,128)(2,1)S(1)} %copy-done), kind=kOutput, calls=%fused_computation.23 | convolution fusion | flops 1207959552 | bytes 6291456 | tf_op jit(solution)/shard_map/dot_general | solution.py:127
  58.0 0.0 copy-start.4
  58.0 0.1 multiply_reduce_fusion.1
  58.1 0.0 copy-done.9
  58.1 0.0 copy-done.10
  58.1 0.8 multiply_multiply_fusion.1
  59.0 0.7 fusion.59
  59.7 0.6 fusion.60
  60.3 0.0 copy-done.4
  60.3 0.7 slice_bitcast_fusion.4
  60.9 6.9 %concatenate.78 = f32[512,1,128]{0,2,1:T(8,128)} concatenate(f32[512,1,8]{0,2,1:T(8,128)} %get-tuple-element.45, f32[512,1,8]{0,2,1:T(8,128)S(1)} %get-tuple-element.44, f32[512,1,28]{0,2,1:T(8,128)} %get-tuple-element.43, f32[512,1,28]{0,2,1:T(8,128)} %get-tuple-element.42, f32[512,1,28]{0,2,1:T(8,128)S(1)} %get-tuple-element.41, f32[512,1,28]{0,2,1:T(8,128)S(1)} %get-tuple-element.40), dimensions={2} | concatenate | bytes 524288 | tf_op jit(solution)/shard_map/concatenate | solution.py:78
  67.8 1.2 add_convert_fusion
  69.0 0.0 copy-start.3
  69.0 1.8 fusion.37
  70.8 3.4 %collective-permute-start = (bf16[1,2,512,1,128]{2,4,1,3,0:T(8,128)(2,1)}, bf16[1,2,512,1,128]{2,4,1,3,0:T(8,128)(2,1)}, u32[]{:S(2)}, u32[]{:S(2)}) collective-permute-start(bf16[1,2,512,1,128]{2,4,1,3,0:T(8,128)(2,1)} %get-tuple-element.36), channel_id=1, source_target_pairs={{0,4},{4,8},{8,12},{12,16},{16,20},{20,24},{24,28},{1,5},{5,9},{9,... | collective-permute-start | bytes 786440 | tf_op jit(solution)/shard_map/ppermute | solution.py:23
  74.2 1.7 fusion.56
  75.9 3.3 %collective-permute-start.1 = (bf16[1,2,512,1,128]{2,4,3,1,0:T(8,128)(2,1)}, bf16[1,2,512,1,128]{2,4,3,1,0:T(8,128)(2,1)}, u32[]{:S(2)}, u32[]{:S(2)}) collective-permute-start(bf16[1,2,512,1,128]{2,4,3,1,0:T(8,128)(2,1)} %get-tuple-element.37), channel_id=1, source_target_pairs={{4,0},{8,4},{12,8},{16,12},{20,16},{24,20},{28,24},{5,1},{9,5},{13... | collective-permute-start | bytes 786440 | tf_op jit(solution)/shard_map/ppermute | solution.py:25
  79.2 1.3 fusion.57
  80.6 1.6 slice.134
  82.2 7.8 %concatenate.77 = f32[512,1,128]{0,2,1:T(8,128)} concatenate(f32[512,1,8]{0,2,1:T(8,128)} %get-tuple-element.35, f32[512,1,8]{0,2,1:T(8,128)S(1)} %get-tuple-element.34, f32[512,1,28]{0,2,1:T(8,128)} %get-tuple-element.33, f32[512,1,28]{0,2,1:T(8,128)} %get-tuple-element.32, f32[512,1,28]{0,2,1:T(8,128)} %get-tuple-element.31, f32[512,1,28]{0,2,1:T(8,128)} %get-tuple-element.30), dimensions={2} | concatenate | bytes 524288 | tf_op jit(solution)/shard_map/concatenate | solution.py:78
  90.0 0.0 collective-permute-done
  90.0 1.7 slice_bitcast_fusion.1
  91.6 0.0 collective-permute-done.1
  91.6 1.6 slice_bitcast_fusion
  93.3 0.0 copy-done.3
  93.3 1.8 fusion.62
  95.1 0.0 copy-start.5
  95.1 1.6 copy-done.1
  96.7 0.6 fusion.6
  97.3 0.0 copy-done.5
  97.3 0.0 copy-done.6
  97.3 0.0 copy-done.7
  97.3 6.0 %convolution_convert_fusion = bf16[512,3072]{1,0:T(8,128)(2,1)} fusion(f32[512,1536]{1,0:T(8,128)} %copy-done.1, f32[512]{0:T(512)S(1)} %fusion.6, f32[512]{0:T(512)S(1)} %get-tuple-element.51, bf16[1,128,3072]{2,1,0:T(8,128)(2,1)} %param.14, bf16[512,1,128]{0,2,1:T(8,128)(2,1)S(1)} %copy-done.7, bf16[512,1,128]{0,2,1:T(8,128)(2,1)S(1)} %copy-done.5, ...), kind=kOutput, calls=%fused_computation.2 | convolution fusion | flops 609157120 | bytes 7475200 | tf_op jit(solution)/shard_map/dot_general | solution.py:163
  103.3 0.0 reduce-scatter.2.cloned.1.call-update
  103.3 0.0 all-reduce.2.cloned.1.call-start
  103.4 37.9 %reduce-scatter.2.cloned.1.call-done = bf16[128,3072]{1,0:T(8,128)(2,1)} async-done(((bf16[512,3072]{1,0:T(8,128)(2,1)}), bf16[128,3072]{1,0:T(8,128)(2,1)}) %reduce-scatter.2.cloned.1.call-update) | async-done | bytes 786448 | tf_op jit(solution)/shard_map/reduce_scatter | solution.py:162
  141.3 2.6 %broadcast_select_fusion = (bf16[128,3072]{1,0:T(8,128)(2,1)}, bf16[128,3072]{1,0:T(8,128)(2,1)}) fusion(pred[]{:T(512)S(6)} %eq.23, bf16[128,3072]{1,0:T(8,128)(2,1)} %reduce-scatter.2.cloned.1.call-done, f32[3072]{0:T(1024)S(1)} %bitcast.87, bf16[1,128,3072]{2,1,0:T(8,128)(2,1)S(1)} %copy-done.2), kind=kLoop, calls=%fused_computation.27 | loop fusion | flops 2359296 | bytes 3158017 | tf_op jit(solution)/shard_map/jit(_where)/select_n | solution.py:40
  143.9 0.0 all-reduce.2.cloned.1.call-update
  143.9 3.4 %collective-permute-start.2 = (bf16[128,3072]{1,0:T(8,128)(2,1)}, bf16[128,3072]{1,0:T(8,128)(2,1)S(1)}, u32[]{:S(2)}, u32[]{:S(2)}) collective-permute-start(bf16[128,3072]{1,0:T(8,128)(2,1)} %get-tuple-element.17), channel_id=1, source_target_pairs={{0,4},{4,8},{8,12},{12,16},{16,20},{20,24},{24,28},{1,5},{5,9},{9,... | collective-permute-start | bytes 2359304 | tf_op jit(solution)/shard_map/ppermute | solution.py:35
  147.3 77.1 %all-reduce.2.cloned.1.call-done = bf16[128,3072]{1,0:T(8,128)(2,1)} async-done(((bf16[128,3072]{1,0:T(8,128)(2,1)}), bf16[128,3072]{1,0:T(8,128)(2,1)}) %all-reduce.2.cloned.1.call-update) | async-done | bytes 786448 | tf_op jit(solution)/shard_map/psum | solution.py:40
  224.4 1.5 constant_dynamic-slice_fusion
  226.0 0.0 collective-permute-done.2
  226.0 1.0 select_bitcast_fusion
  (19 shorter events, 0.1 us)
Async XLA Ops:
  7.2 47.5 %copy-start = (bf16[1,3072,1,384]{3,1,2,0:T(8,128)(2,1)S(1)}, bf16[1,3072,1,384]{3,1,2,0:T(8,128)(2,1)}, u32[]{:S(2)}) copy-start(bf16[1,3072,1,384]{3,1,2,0:T(8,128)(2,1)} %param.13) | copy-start | bytes 7077892
  7.2 47.5 %all-gather.4.cloned.1.call-start = ((), (), s32[]{:S(2)}) async-start(), calls=%async_computation.1 | async-start | bytes 3932160 | tf_op jit(solution)/shard_map/all_gather | solution.py:128
  10.1 12.8 %copy-start.2 = (bf16[1,128,3072]{2,1,0:T(8,128)(2,1)S(1)}, bf16[1,128,3072]{2,1,0:T(8,128)(2,1)}, u32[]{:S(2)}) copy-start(bf16[1,128,3072]{2,1,0:T(8,128)(2,1)} %param.10) | copy-start | bytes 2359300
  24.8 116.5 %reduce-scatter.2.cloned.1.call-start = ((), (), s32[]{:S(2)}) async-start(), calls=%async_computation.2 | async-start | bytes 3932160 | tf_op jit(solution)/shard_map/reduce_scatter | solution.py:162
  28.3 29.8 %copy-start.9 = (f32[1,128]{1,0:T(1,128)S(1)}, f32[1,128]{1,0:T(1,128)}, u32[]{:S(2)}) copy-start(f32[1,128]{1,0:T(1,128)} %param.15) | copy-start | bytes 1540
  28.3 29.8 %copy-start.10 = (f32[1,128]{1,0:T(1,128)S(1)}, f32[1,128]{1,0:T(1,128)}, u32[]{:S(2)}) copy-start(f32[1,128]{1,0:T(1,128)} %param.16) | copy-start | bytes 1540
  58.0 2.2 copy-start.4
  69.0 24.3 %copy-start.3 = (f32[512,1,128]{0,2,1:T(8,128)S(1)}, f32[512,1,128]{0,2,1:T(8,128)}, u32[]{:S(2)}) copy-start(f32[512,1,128]{0,2,1:T(8,128)} %get-tuple-element.24) | copy-start | bytes 786436
  70.8 19.2 %collective-permute-start = (bf16[1,2,512,1,128]{2,4,1,3,0:T(8,128)(2,1)}, bf16[1,2,512,1,128]{2,4,1,3,0:T(8,128)(2,1)}, u32[]{:S(2)}, u32[]{:S(2)}) collective-permute-start(bf16[1,2,512,1,128]{2,4,1,3,0:T(8,128)(2,1)} %get-tuple-element.36), channel_id=1, source_target_pairs={{0,4},{4,8},{8,12},{12,16},{16,20},{20,24},{24,28},{1,5},{5,9},{9,... | collective-permute-start | bytes 786440 | tf_op jit(solution)/shard_map/ppermute | solution.py:23
  75.9 15.8 %collective-permute-start.1 = (bf16[1,2,512,1,128]{2,4,3,1,0:T(8,128)(2,1)}, bf16[1,2,512,1,128]{2,4,3,1,0:T(8,128)(2,1)}, u32[]{:S(2)}, u32[]{:S(2)}) collective-permute-start(bf16[1,2,512,1,128]{2,4,3,1,0:T(8,128)(2,1)} %get-tuple-element.37), channel_id=1, source_target_pairs={{4,0},{8,4},{12,8},{16,12},{20,16},{24,20},{28,24},{5,1},{9,5},{13... | collective-permute-start | bytes 786440 | tf_op jit(solution)/shard_map/ppermute | solution.py:25
  95.1 1.6 copy-start.1
  95.1 2.2 copy-start.5
  95.1 2.2 copy-start.6
  95.1 2.2 copy-start.7
  103.3 38.0 %copy-start.8 = (f32[1,3072]{1,0:T(1,128)S(1)}, f32[1,3072]{1,0:T(1,128)}, u32[]{:S(2)}) copy-start(f32[1,3072]{1,0:T(1,128)} %get-tuple-element.46) | copy-start | bytes 36868
  103.3 121.1 %all-reduce.2.cloned.1.call-start = ((), (), s32[]{:S(2)}) async-start(), calls=%async_computation.3 | async-start | bytes 1572864 | tf_op jit(solution)/shard_map/psum | solution.py:40
  143.9 82.0 %collective-permute-start.2 = (bf16[128,3072]{1,0:T(8,128)(2,1)}, bf16[128,3072]{1,0:T(8,128)(2,1)S(1)}, u32[]{:S(2)}, u32[]{:S(2)}) collective-permute-start(bf16[128,3072]{1,0:T(8,128)(2,1)} %get-tuple-element.17), channel_id=1, source_target_pairs={{0,4},{4,8},{8,12},{12,16},{16,20},{20,24},{24,28},{1,5},{5,9},{9,... | collective-permute-start | bytes 2359304 | tf_op jit(solution)/shard_map/ppermute | solution.py:35
Sparse Core Ops, SparseCore 0:
  24.9 29.7 all-gather.3
  103.4 37.7 reduce-scatter.1
  145.6 78.7 all-reduce.1
where the time goes:
time: 238 us; the launch traced here: 233 us
  waiting for transfers between devices  141 us (59%)
  local copies, waits for them, and re-layouts  25.5 us (11%)
  matrix products  18.1 us (8%)
  other arithmetic  16.9 us (7%)
  between operations  16.1 us (7%)
  starting transfers between devices  10.2 us (4%)
  blocking collectives  5.2 us (2%)
    psum x1, waiting for transfers between devices, broadcast(): return lax.psum(jnp.where(mine, value, jnp.zeros_like(value)), axis)  77.1 us
    reduce_scatter x1, waiting for transfers between devices, shards(): lax.psum_scatter(jnp.dot(attended, w_out[0], preferred_element_type=jnp.f...  37.9 us
    all_gather x1, waiting for transfers between devices, shards(): lax.all_gather(modulated, 'seq', axis=0, tiled=True)  26.4 us
    concatenate x2, local copies, waits for them, and re-layouts, rotate_half(): return jnp.concatenate(pieces_out, axis=-1)  14.7 us
    dot_general x1, matrix products, shards(): mod_part = jnp.dot(embedding, w_mod[0], preferred_element_type=jnp.float32)  7.03 us
    dot_general x1, matrix products, shards(): jnp.dot(attended, w_out[0], preferred_element_type=jnp.float32)  5.99 us
    all_gather x1, blocking collectives, shards(): modulation = lax.all_gather(mod_part, 'seq', axis=1, tiled=True)[0]  5.2 us
  transfers between devices with their start and end apart: 6, of which 3 were waited for; matrix products, arithmetic and copies ran while one was open for 8% of the time, Pallas kernels for 0%

commit v1 on v0

--- a/solution.py
+++ b/solution.py
@@ -1,8 +1,12 @@
+import functools
 import math
 
 import jax
 import jax.numpy as jnp
 from jax import lax
+import numpy as np
+from jax.experimental import pallas as pl
+from jax.experimental.pallas import tpu as pltpu
 from jax.sharding import PartitionSpec as P
 
 GRID_W = 32
@@ -174,6 +178,543 @@
     return (queue_next, clean_frame)
 
 
+MESH = pl.DeviceIdType.MESH
+PEERS = 4
+MOD_CHUNKS = 6
+X_CHUNKS = 4
+OUT_CHUNKS = 4
+LANES = 128
+
+
+def fits(mesh):
+    return mesh.shape["seq"] == PEERS
+
+
+def rope_rows(head_dim):
+    time_dim = head_dim // 8
+    space_dim = (head_dim - time_dim) // 2
+    rows = np.zeros((8, head_dim), np.float32)
+    start = 0
+    for at, section in enumerate((time_dim, space_dim, space_dim)):
+        half = section // 2
+        frequency = ROPE_BASE ** (-2.0 * np.arange(half) / section)
+        rows[at, start : start + half] = frequency
+        rows[at, start + half : start + section] = frequency
+        back, forth = (3, 4) if at == 0 else (5, 6)
+        rows[back, start + half : start + section] = 1.0
+        rows[forth, start : start + half] = -1.0
+        start += section
+    return rows, time_dim // 2, space_dim // 2
+
+
+def time_rates(width):
+    half_width = width // 2
+    return np.exp(-np.log(10000.0) * np.arange(half_width) / half_width).astype(np.float32)[None]
+
+
+def block_kernel(
+    segments,
+    halves,
+    queue,
+    fresh,
+    w_mod,
+    w_qkv,
+    w_out,
+    q_gain,
+    k_gain,
+    levels,
+    plan,
+    positions,
+    rates,
+    rope,
+    queue_next,
+    clean,
+    mod_w,
+    qkv_w,
+    out_w,
+    tokens,
+    mod_all,
+    mod_rows,
+    normed,
+    cosines,
+    sines,
+    queries,
+    kv,
+    own_att,
+    att,
+    done,
+    local_sem,
+    x_send,
+    x_recv,
+    m_send,
+    m_recv,
+    h_send,
+    h_recv,
+    w_send,
+    w_recv,
+    a_send,
+    a_recv,
+    s_send,
+    s_recv,
+    c_send,
+    c_recv,
+):
+    f = lax.axis_index("segment")
+    q = lax.axis_index("seq")
+    last = segments - 1
+    rows, width = queue.shape
+    head_dim = q_gain.shape[1]
+    mod_cols = w_mod.shape[1]
+    peers = (q, q + 1 - 2 * lax.rem(q, 2), lax.rem(q + 2, 4), 3 - q)
+
+    def remote(source, target, send, recv, device):
+        return pltpu.make_async_remote_copy(
+            src_ref=source,
+            dst_ref=target,
+            send_sem=send,
+            recv_sem=recv,
+            device_id=device,
+            device_id_type=MESH,
+        )
+
+    own_tokens = pltpu.make_async_copy(queue, tokens.at[0], local_sem.at[0])
+    own_tokens.start()
+    mod_depth = width // MOD_CHUNKS
+    mod_loads = []
+    for i in range(MOD_CHUNKS):
+        part = pl.ds(i * mod_depth, mod_depth)
+        load = pltpu.make_async_copy(w_mod.at[part], mod_w.at[part], local_sem.at[1 + i])
+        load.start()
+        mod_loads.append(load)
+    qkv_load = pltpu.make_async_copy(w_qkv, qkv_w, local_sem.at[1 + MOD_CHUNKS])
+    qkv_load.start()
+    out_load = pltpu.make_async_copy(w_out, out_w.at[0], local_sem.at[2 + MOD_CHUNKS])
+    out_load.start()
+
+    barrier = pltpu.get_barrier_semaphore()
+    for rel in range(1, PEERS):
+        pl.semaphore_signal(barrier, inc=1, device_id=(f, peers[rel]), device_id_type=MESH)
+    for step in range(1, segments):
+        pl.semaphore_signal(
+            barrier, inc=1, device_id=(lax.rem(f + step, segments), q), device_id_type=MESH
+        )
+    pl.semaphore_wait(barrier, PEERS - 1 + segments - 1)
+
+    piece = rows // X_CHUNKS
+    mirror_x = []
+    for i in range(X_CHUNKS):
+        part = pl.ds(i * piece, piece)
+        copy = remote(
+            queue.at[part], tokens.at[2, part], x_send.at[i], x_recv.at[i], (f, peers[2])
+        )
+        copy.start()
+        mirror_x.append(copy)
+    sibling_x = remote(
+        queue, tokens.at[1], x_send.at[X_CHUNKS], x_recv.at[X_CHUNKS], (f, peers[1])
+    )
+    sibling_x.start()
+    fresh_copy = pltpu.make_async_copy(fresh, queue_next, local_sem.at[3 + MOD_CHUNKS])
+
+    @pl.when(f == 0)
+    def _():
+        fresh_copy.start()
+
+    step_value = plan[levels[0]].astype(jnp.float32)
+    angles = rates[...] * step_value
+    embedding = jnp.concatenate([jnp.cos(angles), jnp.sin(angles)], axis=1)
+    embedding = embedding / (1.0 + jnp.exp(-embedding))
+    embedding = jnp.broadcast_to(embedding, (16, width)).astype(jnp.bfloat16)
+    total = jnp.zeros((16, mod_cols), jnp.float32)
+    for i in range(MOD_CHUNKS):
+        mod_loads[i].wait()
+        total = total + jnp.dot(
+            embedding[:, i * mod_depth : (i + 1) * mod_depth],
+            mod_w[i * mod_depth : (i + 1) * mod_depth, :],
+            preferred_element_type=jnp.float32,
+        )
+    mod_all[q] = total[:1]
+    mod_copies = []
+    for rel in range(1, PEERS):
+        copy = remote(
+            mod_all.at[q], mod_all.at[q], m_send.at[rel], m_recv.at[rel], (f, peers[rel])
+        )
+        copy.start()
+        mod_copies.append(copy)
+
+    position = positions[0].astype(jnp.float32)
+    for rel in range(PEERS):
+        spot = lax.broadcasted_iota(jnp.int32, (rows, head_dim), 0) + peers[rel] * rows
+        grid_row = (spot // GRID_W).astype(jnp.float32)
+        grid_col = (spot % GRID_W).astype(jnp.float32)
+        turn = position * rope[0:1] + grid_row * rope[1:2] + grid_col * rope[2:3]
+        cosines[rel] = jnp.cos(turn)
+        sines[rel] = jnp.sin(turn)
+
+    @pl.when(f == 0)
+    def _():
+        kv[0] = jnp.zeros_like(kv[0])
+
+    @pl.when(f == last)
+    def _():
+        kv[2] = jnp.zeros_like(kv[2])
+
+    own_tokens.wait()
+    qkv_load.wait()
+    out_load.wait()
+    for copy in mod_copies:
+        copy.wait()
+    for peer in range(PEERS):
+        mod_rows[:, peer * mod_cols : (peer + 1) * mod_cols] = mod_all[peer]
+
+    halo = []
+
+    def project(pieces, task):
+        count = len(pieces)
+        at = 0
+        for rel, start, size in pieces:
+
+            def norm_rows(i, carry, rel=rel, start=start, at=at):
+                offset = pl.multiple_of(i * 16, 16)
+                x = tokens[rel, pl.ds(start + offset, 16), :].astype(jnp.float32)
+                x = x - jnp.mean(x, axis=1, keepdims=True)
+                spread = jnp.mean(x * x, axis=1, keepdims=True)
+                x = x * lax.rsqrt(spread + EPSILON)
+                x = x * (1.0 + mod_rows[:, width : 2 * width]) + mod_rows[:, :width]
+                normed[pl.ds(at + offset, 16), :] = x.astype(jnp.bfloat16)
+                return carry
+
+            lax.fori_loop(0, size // 16, norm_rows, 0)
+            at += size
+        joined = jnp.dot(normed[:at, :], qkv_w[...], preferred_element_type=jnp.float32)
+        at = 0
+        for rel, start, size in pieces:
+            cos = cosines[rel, start : start + size, :]
+            sin = sines[rel, start : start + size, :]
+
+            def turned(x, gain):
+                x = x * lax.rsqrt(jnp.mean(x * x, axis=1, keepdims=True) + EPSILON) * gain
+                swapped = (
+                    pltpu.roll(x, halves[0], 1) * rope[3:4]
+                    + pltpu.roll(x, head_dim - halves[0], 1) * rope[4:5]
+                    + pltpu.roll(x, halves[1], 1) * rope[5:6]
+                    + pltpu.roll(x, head_dim - halves[1], 1) * rope[6:7]
+                )
+                return (x * cos + swapped * sin).astype(jnp.bfloat16)
+
+            own = joined[at : at + size]
+            queries[rel, start : start + size, :] = turned(own[:, :head_dim], q_gain[...])
+            kv[1, 0, rel, start : start + size, :] = turned(
+                own[:, head_dim : 2 * head_dim], k_gain[...]
+            )
+            kv[1, 1, rel, start : start + size, :] = own[:, 2 * head_dim :].astype(jnp.bfloat16)
+            at += size
+        rels = pl.ds(pieces[0][0], count)
+        part = pl.ds(pieces[0][1], pieces[0][2])
+        forth = remote(
+            kv.at[1, :, rels, part],
+            kv.at[0, :, rels, part],
+            h_send.at[0, task],
+            h_recv.at[0, task],
+            (lax.rem(f + 1, segments), q),
+        )
+        back = remote(
+            kv.at[1, :, rels, part],
+            kv.at[2, :, rels, part],
+            h_send.at[1, task],
+            h_recv.at[1, task],
+            (lax.rem(f + segments - 1, segments), q),
+        )
+
+        @pl.when(f < last)
+        def _():
+            forth.start()
+
+        @pl.when(f > 0)
+        def _():
+            back.start()
+
+        halo.append((forth, back))
+
+    forwards = []
+
+    def forward_tokens(i):
+        mirror_x[i].wait_recv()
+        part = pl.ds(i * piece, piece)
+        copy = remote(
+            tokens.at[2, part],
+            tokens.at[3, part],
+            x_send.at[X_CHUNKS + 1 + i],
+            x_recv.at[X_CHUNKS + 1 + i],
+            (f, peers[1]),
+        )
+        copy.start()
+        forwards.append(copy)
+
+    sibling_x.wait_recv()
+    project([(0, 0, rows), (1, 0, rows)], 0)
+    half = rows // 2
+    for i in range(X_CHUNKS // 2):
+        forward_tokens(i)
+    for i in range(X_CHUNKS // 2):
+        forwards[i].wait_recv()
+    project([(2, 0, half), (3, 0, half)], 1)
+    for i in range(X_CHUNKS // 2, X_CHUNKS):
+        forward_tokens(i)
+
+    cols = width // OUT_CHUNKS
+    mirror_w = []
+    for i in range(OUT_CHUNKS):
+        part = pl.ds(i * cols, cols)
+        copy = remote(
+            out_w.at[0, :, part],
+            out_w.at[2, :, part],
+            w_send.at[i],
+            w_recv.at[i],
+            (f, peers[2]),
+        )
+        copy.start()
+        mirror_w.append(copy)
+    sibling_w = remote(
+        out_w.at[0], out_w.at[1], w_send.at[OUT_CHUNKS], w_recv.at[OUT_CHUNKS], (f, peers[1])
+    )
+    for i in range(X_CHUNKS // 2, X_CHUNKS):
+        forwards[i].wait_recv()
+    project([(2, half, half), (3, half, half)], 2)
+    sibling_w.start()
+
+    for forth, back in halo:
+
+        @pl.when(f > 0)
+        def _(forth=forth):
+            forth.wait_recv()
+
+        @pl.when(f < last)
+        def _(back=back):
+            back.wait_recv()
+
+    scale = head_dim ** (-0.5)
+    tokens_all = PEERS * rows
+    att_copies = []
+    for rel in (3, 2, 1, 0):
+        query_rows = queries[rel]
+        scores = []
+        for side in range(3):
+            key_rows = kv[side, 0].reshape(tokens_all, head_dim)
+            part = (
+                lax.dot_general(
+                    query_rows,
+                    key_rows,
+                    (((1,), (1,)), ((), ())),
+                    preferred_element_type=jnp.float32,
+                )
+                * scale
+            )
+            if side == 0:
+                part = jnp.where(f > 0, part, -jnp.inf)
+            if side == 2:
+                part = jnp.where(f < last, part, -jnp.inf)
+            scores.append(part)
+        top = jnp.maximum(
+            jnp.max(jnp.maximum(scores[0], scores[2]), axis=1, keepdims=True),
+            jnp.max(scores[1], axis=1, keepdims=True),
+        )
+        weight = jnp.zeros((rows, 1), jnp.float32)
+        mixed = jnp.zeros((rows, head_dim), jnp.float32)
+        for side in range(3):
+            raised = jnp.exp(scores[side] - top)
+            weight = weight + jnp.sum(raised, axis=1, keepdims=True)
+            mixed = mixed + jnp.dot(
+                raised.astype(jnp.bfloat16),
+                kv[side, 1].reshape(tokens_all, head_dim),
+                preferred_element_type=jnp.float32,
+            )
+        mixed = (mixed / weight).astype(jnp.bfloat16)
+        if rel == 0:
+            att[0] = mixed
+        else:
+            own_att[rel] = mixed
+            copy = remote(
+                own_att.at[rel], att.at[rel], a_send.at[rel], a_recv.at[rel], (f, peers[rel])
+            )
+            copy.start()
+            att_copies.append(copy)
+
+    forward_w = []
+
+    def forward_weights(i):
+        mirror_w[i].wait_recv()
+        part = pl.ds(i * cols, cols)
+        copy = remote(
+            out_w.at[2, :, part],
+            out_w.at[3, :, part],
+            w_send.at[OUT_CHUNKS + 1 + i],
+            w_recv.at[OUT_CHUNKS + 1 + i],
+            (f, peers[1]),
+        )
+        copy.start()
+        forward_w.append(copy)
+
+    forward_weights(0)
+    sibling_w.wait_recv()
+    for copy in att_copies:
+        copy.wait_recv()
+    mixed = jnp.concatenate([att[rel] for rel in range(PEERS)], axis=1)
+
+    clean_cols = width // segments
+    shifts = []
+    cleans = []
+    for i in range(OUT_CHUNKS):
+        if i + 1 < OUT_CHUNKS:
+            forward_weights(i + 1)
+        forward_w[i].wait_recv()
+        begin = i * cols
+        part = pl.ds(begin, cols)
+        projected = jnp.dot(
+            mixed,
+            out_w[:, :, begin : begin + cols].reshape(PEERS * rows, cols),
+            preferred_element_type=jnp.float32,
+        )
+        gate = mod_rows[:, 2 * width + begin : 2 * width + begin + cols]
+        kept = tokens[0, :, begin : begin + cols].astype(jnp.float32)
+        done[:, begin : begin + cols] = (kept + gate * projected).astype(jnp.bfloat16)
+        shift = remote(
+            done.at[:, part],
+            queue_next.at[:, part],
+            s_send.at[i],
+            s_recv.at[i],
+            (lax.rem(f + 1, segments), q),
+        )
+        shifts.append(shift)
+
+        @pl.when(f < last)
+        def _(shift=shift):
+            shift.start()
+
+        for to in range(begin // clean_cols, (begin + cols) // clean_cols):
+            from_cols = done.at[:, pl.ds(to * clean_cols, clean_cols)]
+            if to < last:
+                clean_copy = remote(from_cols, clean, c_send.at[to], c_recv, (to, q))
+            else:
+                clean_copy = pltpu.make_async_copy(from_cols, clean, c_send.at[to])
+            cleans.append(clean_copy)
+
+            @pl.when(f == last)
+            def _(clean_copy=clean_copy):
+                clean_copy.start()
+
+    for copy in mirror_x + [sibling_x] + forwards + mirror_w + [sibling_w] + forward_w + att_copies:
+        copy.wait_send()
+    for forth, back in halo:
+
+        @pl.when(f < last)
+        def _(forth=forth):
+            forth.wait_send()
+
+        @pl.when(f > 0)
+        def _(back=back):
+            back.wait_send()
+
+    @pl.when(f == 0)
+    def _():
+        fresh_copy.wait()
+
+    for shift in shifts:
+
+        @pl.when(f < last)
+        def _(shift=shift):
+            shift.wait_send()
+
+        @pl.when(f > 0)
+        def _(shift=shift):
+            shift.wait_recv()
+
+    @pl.when(f == last)
+    def _():
+        for clean_copy in cleans[:-1]:
+            clean_copy.wait_send()
+        cleans[-1].wait()
+
+    @pl.when(f < last)
+    def _():
+        cleans[0].wait_recv()
+
+
+def fused(
+    mesh, queue, fresh_noise, w_mod, w_qkv, w_out, q_gain, k_gain, levels, plan, positions
+):
+    segments = mesh.shape["segment"]
+    rows, width = queue.shape[1:]
+    mod_cols = w_mod.shape[2]
+    head_dim = q_gain.shape[1]
+    rope, *halves = rope_rows(head_dim)
+    whole = pl.BlockSpec(memory_space=pltpu.VMEM)
+    scalars = pl.BlockSpec(memory_space=pltpu.SMEM)
+    outside = pl.BlockSpec(memory_space=pl.ANY)
+    bf16, f32 = jnp.bfloat16, jnp.float32
+    dma = pltpu.SemaphoreType.DMA
+    queue_next, clean_frame = pl.pallas_call(
+        functools.partial(block_kernel, segments, tuple(halves)),
+        out_shape=(
+            jax.ShapeDtypeStruct((rows, width), bf16),
+            jax.ShapeDtypeStruct((rows, width // segments), bf16),
+        ),
+        in_specs=[outside] * 5 + [whole] * 2 + [scalars] * 3 + [whole] * 2,
+        out_specs=(outside, outside),
+        scratch_shapes=[
+            pltpu.VMEM((width, mod_cols), bf16),
+            pltpu.VMEM((width, 3 * head_dim), bf16),
+            pltpu.VMEM((PEERS, rows, width), bf16),
+            pltpu.VMEM((PEERS, rows, width), bf16),
+            pltpu.VMEM((PEERS, 1, mod_cols), f32),
+            pltpu.VMEM((1, 3 * width), f32),
+            pltpu.VMEM((2 * rows, width), bf16),
+            pltpu.VMEM((PEERS, rows, head_dim), f32),
+            pltpu.VMEM((PEERS, rows, head_dim), f32),
+            pltpu.VMEM((PEERS, rows, head_dim), bf16),
+            pltpu.VMEM((3, 2, PEERS, rows, head_dim), bf16),
+            pltpu.VMEM((PEERS, rows, head_dim), bf16),
+            pltpu.VMEM((PEERS, rows, head_dim), bf16),
+            pltpu.VMEM((rows, width), bf16),
+            dma((4 + MOD_CHUNKS,)),
+            dma((2 * X_CHUNKS + 1,)),
+            dma((2 * X_CHUNKS + 1,)),
+            dma((PEERS,)),
+            dma((PEERS,)),
+            dma((2, 3)),
+            dma((2, 3)),
+            dma((2 * OUT_CHUNKS + 1,)),
+            dma((2 * OUT_CHUNKS + 1,)),
+            dma((PEERS,)),
+            dma((PEERS,)),
+            dma((OUT_CHUNKS,)),
+            dma((OUT_CHUNKS,)),
+            dma((segments,)),
+            dma(()),
+        ],
+        compiler_params=pltpu.CompilerParams(
+            collective_id=0, has_side_effects=True, vmem_limit_bytes=56 * 1024 * 1024
+        ),
+        cost_estimate=pl.CostEstimate(
+            flops=2 * 10**9, bytes_accessed=22 * 10**6, transcendentals=10**6
+        ),
+        name="relayed_block",
+    )(
+        queue[0],
+        fresh_noise,
+        w_mod[0],
+        w_qkv.reshape(width, 3 * head_dim),
+        w_out[0],
+        q_gain,
+        k_gain,
+        levels,
+        plan,
+        positions,
+        jnp.asarray(time_rates(width)),
+        jnp.asarray(rope),
+    )
+    return queue_next[None], clean_frame
+
+
 def solution(mesh):
     placed = (
         P("segment", "seq", None),
@@ -188,7 +729,7 @@
         P("segment"),
     )
     return jax.shard_map(
-        shards,
+        functools.partial(fused, mesh) if fits(mesh) else shards,
         mesh=mesh,
         in_specs=placed,
         out_specs=(P("segment", "seq", None), P("seq", "segment")),

time: 238 us -> 81.2 us (0.34); the launches traced: 233 us -> 81 us
  waiting for transfers between devices: 141 us -> 0 us
  Pallas kernels: 0 us -> 75.4 us
  local copies, waits for them, and re-layouts: 25.5 us -> 3.61 us
  matrix products: 18.1 us -> 0 us
  other arithmetic: 16.9 us -> 0 us
  between operations: 16.1 us -> 1.93 us
  starting transfers between devices: 10.2 us -> 0 us
  blocking collectives: 5.2 us -> 0 us
    psum x1 -> x0, waiting for transfers between devices: 77.1 us -> none  [broadcast(): return lax.psum(jnp.where(mine, value, jnp.zeros_like(value)), axis)]
    pallas_call x0 -> x1, Pallas kernels: none -> 75.4 us  [fused(): pl.pallas_call(functools.partial(block_kernel, segments, tuple(halves)),...]
    reduce_scatter x1 -> x0, waiting for transfers between devices: 37.9 us -> none  [shards(): lax.psum_scatter(jnp.dot(attended, w_out[0], preferred_element_type=jnp.f...]
    all_gather x1 -> x0, waiting for transfers between devices: 26.4 us -> none  [shards(): lax.all_gather(modulated, 'seq', axis=0, tiled=True)]
    dot_general x4 -> x0, matrix products: 18.1 us -> none  [the longest x1 7.03 us: shards(): mod_part = jnp.dot(embedding, w_mod[0], preferred_element_type=jnp.float32)]
    concatenate x4 -> x0, local copies, waits for them, and re-layouts: 15.1 us -> none  [the longest x2 14.7 us: rotate_half(): return jnp.concatenate(pieces_out, axis=-1)]
    ppermute x3 -> x0, starting transfers between devices: 10.1 us -> none  [the longest x1 3.38 us: passed_along(): return lax.ppermute(value, axis, pairs)]
    all_gather x1 -> x0, blocking collectives: 5.2 us -> none  [shards(): modulation = lax.all_gather(mod_part, 'seq', axis=1, tiled=True)[0]]
  transfers between devices with their start and end apart: 6 -> 0, of which waited for: 3 -> 0; matrix products, arithmetic and copies ran while one was open for 8% -> 0% of each run, Pallas kernels for 0% -> 0%
where the time goes in v1:
time: 81.2 us; the launch traced here: 81 us
  Pallas kernels  75.4 us (93%)
  local copies, waits for them, and re-layouts  3.61 us (4%)
  between operations  1.93 us (2%)
    pallas_call x1, Pallas kernels, fused(): pl.pallas_call(functools.partial(block_kernel, segments, tuple(halves)),...  75.4 us
    unnamed x2, local copies, waits for them, and re-layouts  3.61 us

profile of v1, /device:TPU:8, one launch (start us, length us, event | category | flops | bytes accessed | tf_op | source)
XLA Modules:
  0.0 81.0 jit_solution(18296182330554872001)
XLA Ops:
  1.9 75.4 %relayed_block.1 = (bf16[128,3072]{1,0:T(8,128)(2,1)}, bf16[128,384]{1,0:T(8,128)(2,1)}) custom-call(bf16[128,3072]{1,0:T(8,128)(2,1)} %bitcast.7, bf16[128,3072]{1,0:T(8,128)(2,1)} %fresh.1, bf16[3072,2304]{1,0:T(8,128)(2,1)} %bitcast.5, bf16[3072,384]{1,0:T(8,128)(2,1)} %bitcast.6, bf16[128,3072]{1,0:T(8,128)(2,1)} %bitcast.8, f32[1,128]{1,0:T(1,128)} %q_gain.1, ...), custom_call_target="tpu_custom_call" | custom-call | flops 2000000000 | bytes 22000000 | tf_op jit(solution)/shard_map/relayed_block/pallas_call | solution.py:655
  77.4 2.1 %copy.18 = bf16[1,128,3072]{2,1,0:T(8,128)(2,1)} copy(bf16[1,128,3072]{2,1,0:T(8,128)(2,1)} %bitcast.9) | data formatting | bytes 1572864
  79.4 1.5 %copy.19 = bf16[128,384]{1,0:T(8,128)(2,1)} copy(bf16[128,384]{1,0:T(8,128)(2,1)} %get-tuple-element.9) | data formatting | bytes 196608

commit v2 on v1

--- a/solution.py
+++ b/solution.py
@@ -220,13 +220,13 @@
     w_mod,
     w_qkv,
     w_out,
-    q_gain,
-    k_gain,
+    q_gain_in,
+    k_gain_in,
     levels,
     plan,
     positions,
-    rates,
-    rope,
+    rates_in,
+    rope_in,
     queue_next,
     clean,
     mod_w,
@@ -235,6 +235,12 @@
     tokens,
     mod_all,
     mod_rows,
+    rates,
+    rope,
+    q_gain,
+    k_gain,
+    embedded,
+    settled,
     normed,
     cosines,
     sines,
@@ -243,6 +249,7 @@
     own_att,
     att,
     done,
+    small_sem,
     local_sem,
     x_send,
     x_recv,
@@ -263,7 +270,7 @@
     q = lax.axis_index("seq")
     last = segments - 1
     rows, width = queue.shape
-    head_dim = q_gain.shape[1]
+    head_dim = q_gain_in.shape[1]
     mod_cols = w_mod.shape[1]
     peers = (q, q + 1 - 2 * lax.rem(q, 2), lax.rem(q + 2, 4), 3 - q)
 
@@ -277,6 +284,21 @@
             device_id_type=MESH,
         )
 
+    barrier = pltpu.get_barrier_semaphore()
+    for rel in range(1, PEERS):
+        pl.semaphore_signal(barrier, inc=1, device_id=(f, peers[rel]), device_id_type=MESH)
+    for step in range(1, segments):
+        pl.semaphore_signal(
+            barrier, inc=1, device_id=(lax.rem(f + step, segments), q), device_id_type=MESH
+        )
+
+    small_loads = []
+    for i, (source, target) in enumerate(
+        ((rates_in, rates), (rope_in, rope), (q_gain_in, q_gain), (k_gain_in, k_gain))
+    ):
+        load = pltpu.make_async_copy(source, target, small_sem.at[i])
+        load.start()
+        small_loads.append(load)
     own_tokens = pltpu.make_async_copy(queue, tokens.at[0], local_sem.at[0])
     own_tokens.start()
     mod_depth = width // MOD_CHUNKS
@@ -291,13 +313,6 @@
     out_load = pltpu.make_async_copy(w_out, out_w.at[0], local_sem.at[2 + MOD_CHUNKS])
     out_load.start()
 
-    barrier = pltpu.get_barrier_semaphore()
-    for rel in range(1, PEERS):
-        pl.semaphore_signal(barrier, inc=1, device_id=(f, peers[rel]), device_id_type=MESH)
-    for step in range(1, segments):
-        pl.semaphore_signal(
-            barrier, inc=1, device_id=(lax.rem(f + step, segments), q), device_id_type=MESH
-        )
     pl.semaphore_wait(barrier, PEERS - 1 + segments - 1)
 
     piece = rows // X_CHUNKS
@@ -319,20 +334,36 @@
     def _():
         fresh_copy.start()
 
+    for load in small_loads:
+        load.wait()
     step_value = plan[levels[0]].astype(jnp.float32)
     angles = rates[...] * step_value
     embedding = jnp.concatenate([jnp.cos(angles), jnp.sin(angles)], axis=1)
     embedding = embedding / (1.0 + jnp.exp(-embedding))
-    embedding = jnp.broadcast_to(embedding, (16, width)).astype(jnp.bfloat16)
-    total = jnp.zeros((16, mod_cols), jnp.float32)
+    embedding = embedding.astype(jnp.bfloat16).astype(jnp.float32)
+    for start in range(0, width, LANES):
+        entries = jnp.broadcast_to(embedding[:, start : start + LANES], (LANES, LANES))
+        embedded[start : start + LANES, :] = entries.T
+    tiles = mod_cols // LANES
+
+    def add_rows(i, totals):
+        offset = pl.multiple_of(i * 16, 16)
+        entries = embedded[pl.ds(offset, 16), :]
+        sums = []
+        for tile in range(tiles):
+            lanes = slice(tile * LANES, (tile + 1) * LANES)
+            product = mod_w[pl.ds(offset, 16), lanes].astype(jnp.float32) * entries
+            sums.append(totals[tile] + (product[:8] + product[8:]))
+        return tuple(sums)
+
+    totals = tuple(jnp.zeros((8, LANES), jnp.float32) for _ in range(tiles))
+    steps = mod_depth // 16
     for i in range(MOD_CHUNKS):
         mod_loads[i].wait()
-        total = total + jnp.dot(
-            embedding[:, i * mod_depth : (i + 1) * mod_depth],
-            mod_w[i * mod_depth : (i + 1) * mod_depth, :],
-            preferred_element_type=jnp.float32,
-        )
-    mod_all[q] = total[:1]
+        totals = lax.fori_loop(i * steps, (i + 1) * steps, add_rows, totals, unroll=4)
+    mod_all[q] = jnp.concatenate(
+        [jnp.sum(total, axis=0, keepdims=True) for total in totals], axis=1
+    )
     mod_copies = []
     for rel in range(1, PEERS):
         copy = remote(
@@ -342,49 +373,87 @@
         mod_copies.append(copy)
 
     position = positions[0].astype(jnp.float32)
+    grid_col = lax.broadcasted_iota(jnp.int32, (GRID_W, head_dim), 0).astype(jnp.float32)
+    col_turn = grid_col * rope[2:3]
+    col_cos = jnp.cos(col_turn)
+    col_sin = jnp.sin(col_turn)
+    by_col = lax.broadcasted_iota(jnp.int32, (GRID_W, head_dim), 1) >= head_dim - 2 * halves[1]
+    rows_here = rows // GRID_W
     for rel in range(PEERS):
-        spot = lax.broadcasted_iota(jnp.int32, (rows, head_dim), 0) + peers[rel] * rows
-        grid_row = (spot // GRID_W).astype(jnp.float32)
-        grid_col = (spot % GRID_W).astype(jnp.float32)
-        turn = position * rope[0:1] + grid_row * rope[1:2] + grid_col * rope[2:3]
-        cosines[rel] = jnp.cos(turn)
-        sines[rel] = jnp.sin(turn)
-
-    @pl.when(f == 0)
-    def _():
-        kv[0] = jnp.zeros_like(kv[0])
-
-    @pl.when(f == last)
-    def _():
-        kv[2] = jnp.zeros_like(kv[2])
+        grid_row = lax.broadcasted_iota(jnp.int32, (8, head_dim), 0) + peers[rel] * rows_here
+        row_turn = position * rope[0:1] + grid_row.astype(jnp.float32) * rope[1:2]
+        row_cos = jnp.cos(row_turn)
+        row_sin = jnp.sin(row_turn)
+        for r in range(rows_here):
+            part = slice(r * GRID_W, (r + 1) * GRID_W)
+            cosines[rel, part, :] = jnp.where(by_col, col_cos, row_cos[r : r + 1])
+            sines[rel, part, :] = jnp.where(by_col, col_sin, row_sin[r : r + 1])
+
+    forwards = []
+
+    def forward_tokens(i):
+        mirror_x[i].wait_recv()
+        part = pl.ds(i * piece, piece)
+        copy = remote(
+            tokens.at[2, part],
+            tokens.at[3, part],
+            x_send.at[X_CHUNKS + 1 + i],
+            x_recv.at[X_CHUNKS + 1 + i],
+            (f, peers[1]),
+        )
+        copy.start()
+        forwards.append(copy)
+
+    def settle(x):
+        x = x.astype(jnp.float32)
+        x = x - jnp.mean(x, axis=1, keepdims=True)
+        return x * lax.rsqrt(jnp.mean(x * x, axis=1, keepdims=True) + EPSILON)
+
+    def modulate(x):
+        return (x * mod_rows[:, width : 2 * width] + mod_rows[:, :width]).astype(jnp.bfloat16)
 
     own_tokens.wait()
+    forward_tokens(0)
+    sibling_x.wait_recv()
+    for rel in range(2):
+
+        def settle_rows(i, carry, rel=rel):
+            offset = pl.multiple_of(i * 16, 16)
+            settled[pl.ds(rel * rows + offset, 16), :] = settle(tokens[rel, pl.ds(offset, 16), :])
+            return carry
+
+        lax.fori_loop(0, rows // 16, settle_rows, 0, unroll=4)
+    forward_tokens(1)
     qkv_load.wait()
     out_load.wait()
     for copy in mod_copies:
         copy.wait()
     for peer in range(PEERS):
         mod_rows[:, peer * mod_cols : (peer + 1) * mod_cols] = mod_all[peer]
-
+    mod_rows[:, width : 2 * width] = 1.0 + mod_rows[:, width : 2 * width]
+
+    def modulate_rows(i, carry):
+        offset = pl.multiple_of(i * 16, 16)
+        normed[pl.ds(offset, 16), :] = modulate(settled[pl.ds(offset, 16), :])
+        return carry
+
+    lax.fori_loop(0, 2 * rows // 16, modulate_rows, 0, unroll=4)
+
+    def norm_piece(rel, start, size, at):
+        def norm_rows(i, carry):
+            offset = pl.multiple_of(i * 16, 16)
+            x = settle(tokens[rel, pl.ds(start + offset, 16), :])
+            normed[pl.ds(at + offset, 16), :] = modulate(x)
+            return carry
+
+        lax.fori_loop(0, size // 16, norm_rows, 0, unroll=True)
+
+    score_scale = head_dim ** (-0.5) * math.log2(math.e)
     halo = []
 
     def project(pieces, task):
         count = len(pieces)
-        at = 0
-        for rel, start, size in pieces:
-
-            def norm_rows(i, carry, rel=rel, start=start, at=at):
-                offset = pl.multiple_of(i * 16, 16)
-                x = tokens[rel, pl.ds(start + offset, 16), :].astype(jnp.float32)
-                x = x - jnp.mean(x, axis=1, keepdims=True)
-                spread = jnp.mean(x * x, axis=1, keepdims=True)
-                x = x * lax.rsqrt(spread + EPSILON)
-                x = x * (1.0 + mod_rows[:, width : 2 * width]) + mod_rows[:, :width]
-                normed[pl.ds(at + offset, 16), :] = x.astype(jnp.bfloat16)
-                return carry
-
-            lax.fori_loop(0, size // 16, norm_rows, 0)
-            at += size
+        at = sum(size for _, _, size in pieces)
         joined = jnp.dot(normed[:at, :], qkv_w[...], preferred_element_type=jnp.float32)
         at = 0
         for rel, start, size in pieces:
@@ -402,7 +471,9 @@
                 return (x * cos + swapped * sin).astype(jnp.bfloat16)
 
             own = joined[at : at + size]
-            queries[rel, start : start + size, :] = turned(own[:, :head_dim], q_gain[...])
+            queries[rel, start : start + size, :] = turned(
+                own[:, :head_dim], q_gain[...] * score_scale
+            )
             kv[1, 0, rel, start : start + size, :] = turned(
                 own[:, head_dim : 2 * head_dim], k_gain[...]
             )
@@ -435,35 +506,10 @@
 
         halo.append((forth, back))
 
-    forwards = []
-
-    def forward_tokens(i):
-        mirror_x[i].wait_recv()
-        part = pl.ds(i * piece, piece)
-        copy = remote(
-            tokens.at[2, part],
-            tokens.at[3, part],
-            x_send.at[X_CHUNKS + 1 + i],
-            x_recv.at[X_CHUNKS + 1 + i],
-            (f, peers[1]),
-        )
-        copy.start()
-        forwards.append(copy)
-
-    sibling_x.wait_recv()
-    project([(0, 0, rows), (1, 0, rows)], 0)
-    half = rows // 2
-    for i in range(X_CHUNKS // 2):
-        forward_tokens(i)
-    for i in range(X_CHUNKS // 2):
-        forwards[i].wait_recv()
-    project([(2, 0, half), (3, 0, half)], 1)
-    for i in range(X_CHUNKS // 2, X_CHUNKS):
-        forward_tokens(i)
-
     cols = width // OUT_CHUNKS
     mirror_w = []
-    for i in range(OUT_CHUNKS):
+
+    def send_weights(i):
         part = pl.ds(i * cols, cols)
         copy = remote(
             out_w.at[0, :, part],
@@ -474,13 +520,41 @@
         )
         copy.start()
         mirror_w.append(copy)
+
     sibling_w = remote(
         out_w.at[0], out_w.at[1], w_send.at[OUT_CHUNKS], w_recv.at[OUT_CHUNKS], (f, peers[1])
     )
-    for i in range(X_CHUNKS // 2, X_CHUNKS):
+    project([(0, 0, rows), (1, 0, rows)], 0)
+    half = rows // 2
+    forward_tokens(2)
+    send_weights(0)
+    for i in range(2):
         forwards[i].wait_recv()
+        norm_piece(2, i * piece, piece, i * piece)
+        norm_piece(3, i * piece, piece, half + i * piece)
+    project([(2, 0, half), (3, 0, half)], 1)
+    send_weights(1)
+    norm_piece(2, half, piece, 0)
+    forwards[2].wait_recv()
+    norm_piece(3, half, piece, half)
+    forward_tokens(3)
+    send_weights(2)
+    send_weights(3)
+    norm_piece(2, half + piece, piece, piece)
+    forwards[3].wait_recv()
+    norm_piece(3, half + piece, piece, half + piece)
     project([(2, half, half), (3, half, half)], 2)
     sibling_w.start()
+
+    @pl.when(f == 0)
+    def _():
+        kv[0, 0] = kv[1, 0]
+        kv[0, 1] = jnp.zeros_like(kv[0, 1])
+
+    @pl.when(f == last)
+    def _():
+        kv[2, 0] = kv[1, 0]
+        kv[2, 1] = jnp.zeros_like(kv[2, 1])
 
     for forth, back in halo:
 
@@ -492,7 +566,11 @@
         def _(back=back):
             back.wait_recv()
 
-    scale = head_dim ** (-0.5)
+    counted = (
+        jnp.where(f > 0, 1.0, 0.0).astype(jnp.float32),
+        jnp.float32(1.0),
+        jnp.where(f < last, 1.0, 0.0).astype(jnp.float32),
+    )
     tokens_all = PEERS * rows
     att_copies = []
     for rel in (3, 2, 1, 0):
@@ -500,20 +578,14 @@
         scores = []
         for side in range(3):
             key_rows = kv[side, 0].reshape(tokens_all, head_dim)
-            part = (
+            scores.append(
                 lax.dot_general(
                     query_rows,
                     key_rows,
                     (((1,), (1,)), ((), ())),
                     preferred_element_type=jnp.float32,
                 )
-                * scale
             )
-            if side == 0:
-                part = jnp.where(f > 0, part, -jnp.inf)
-            if side == 2:
-                part = jnp.where(f < last, part, -jnp.inf)
-            scores.append(part)
         top = jnp.maximum(
             jnp.max(jnp.maximum(scores[0], scores[2]), axis=1, keepdims=True),
             jnp.max(scores[1], axis=1, keepdims=True),
@@ -521,8 +593,8 @@
         weight = jnp.zeros((rows, 1), jnp.float32)
         mixed = jnp.zeros((rows, head_dim), jnp.float32)
         for side in range(3):
-            raised = jnp.exp(scores[side] - top)
-            weight = weight + jnp.sum(raised, axis=1, keepdims=True)
+            raised = jnp.exp2(scores[side] - top)
+            weight = weight + counted[side] * jnp.sum(raised, axis=1, keepdims=True)
             mixed = mixed + jnp.dot(
                 raised.astype(jnp.bfloat16),
                 kv[side, 1].reshape(tokens_all, head_dim),
@@ -639,6 +711,17 @@
         cleans[0].wait_recv()
 
 
+def hand_over(queue_in, clean_in, queue_next, clean, sem):
+    copies = [
+        pltpu.make_async_copy(queue_in, queue_next, sem.at[0]),
+        pltpu.make_async_copy(clean_in, clean, sem.at[1]),
+    ]
+    for copy in copies:
+        copy.start()
+    for copy in copies:
+        copy.wait()
+
+
 def fused(
     mesh, queue, fresh_noise, w_mod, w_qkv, w_out, q_gain, k_gain, levels, plan, positions
 ):
@@ -647,7 +730,6 @@
     mod_cols = w_mod.shape[2]
     head_dim = q_gain.shape[1]
     rope, *halves = rope_rows(head_dim)
-    whole = pl.BlockSpec(memory_space=pltpu.VMEM)
     scalars = pl.BlockSpec(memory_space=pltpu.SMEM)
     outside = pl.BlockSpec(memory_space=pl.ANY)
     bf16, f32 = jnp.bfloat16, jnp.float32
@@ -658,7 +740,7 @@
             jax.ShapeDtypeStruct((rows, width), bf16),
             jax.ShapeDtypeStruct((rows, width // segments), bf16),
         ),
-        in_specs=[outside] * 5 + [whole] * 2 + [scalars] * 3 + [whole] * 2,
+        in_specs=[outside] * 7 + [scalars] * 3 + [outside] * 2,
         out_specs=(outside, outside),
         scratch_shapes=[
             pltpu.VMEM((width, mod_cols), bf16),
@@ -667,6 +749,12 @@
             pltpu.VMEM((PEERS, rows, width), bf16),
             pltpu.VMEM((PEERS, 1, mod_cols), f32),
             pltpu.VMEM((1, 3 * width), f32),
+            pltpu.VMEM((1, width // 2), f32),
+            pltpu.VMEM((8, head_dim), f32),
+            pltpu.VMEM((1, head_dim), f32),
+            pltpu.VMEM((1, head_dim), f32),
+            pltpu.VMEM((width, LANES), f32),
+            pltpu.VMEM((2 * rows, width), f32),
             pltpu.VMEM((2 * rows, width), bf16),
             pltpu.VMEM((PEERS, rows, head_dim), f32),
             pltpu.VMEM((PEERS, rows, head_dim), f32),
@@ -675,6 +763,7 @@
             pltpu.VMEM((PEERS, rows, head_dim), bf16),
             pltpu.VMEM((PEERS, rows, head_dim), bf16),
             pltpu.VMEM((rows, width), bf16),
+            dma((4,)),
             dma((4 + MOD_CHUNKS,)),
             dma((2 * X_CHUNKS + 1,)),
             dma((2 * X_CHUNKS + 1,)),
@@ -712,6 +801,18 @@
         jnp.asarray(time_rates(width)),
         jnp.asarray(rope),
     )
+    queue_next, clean_frame = pl.pallas_call(
+        hand_over,
+        out_shape=(
+            jax.ShapeDtypeStruct(queue_next.shape, bf16),
+            jax.ShapeDtypeStruct(clean_frame.shape, bf16),
+        ),
+        in_specs=[outside] * 2,
+        out_specs=(outside, outside),
+        scratch_shapes=[dma((2,))],
+        compiler_params=pltpu.CompilerParams(vmem_limit_bytes=56 * 1024 * 1024),
+        name="hand_over",
+    )(queue_next, clean_frame)
     return queue_next[None], clean_frame
 
 

time: 81.2 us -> 97 us (1.19)
  Pallas kernels: 75.4 us -> 94.9 us
  local copies, waits for them, and re-layouts: 3.61 us -> 0 us
    pallas_call x0 -> x1, Pallas kernels: none -> 27.9 us  [fused(): pl.pallas_call(hand_over, out_shape=(jax.ShapeDtypeStruct(queue_next.shap...]
    pallas_call x1, Pallas kernels: 75.4 us -> 67 us  [fused(): pl.pallas_call(functools.partial(block_kernel, segments, tuple(halves)),...]
    unnamed x2 -> x0, local copies, waits for them, and re-layouts: 3.61 us -> none
where the time goes in v2:
time: 97 us; the launch traced here: 96.9 us
  Pallas kernels  94.9 us (98%)
  between operations  1.93 us (2%)
    pallas_call x1, Pallas kernels, fused(): pl.pallas_call(functools.partial(block_kernel, segments, tuple(halves)),...  67 us
    pallas_call x1, Pallas kernels, fused(): pl.pallas_call(hand_over, out_shape=(jax.ShapeDtypeStruct(queue_next.shap...  27.9 us

profile of v2, /device:TPU:8, one launch (start us, length us, event | category | flops | bytes accessed | tf_op | source)
XLA Modules:
  0.0 96.9 jit_solution(6286307974119554894)
XLA Ops:
  1.9 67.0 %relayed_block.1 = (bf16[128,3072]{1,0:T(8,128)(2,1)}, bf16[128,384]{1,0:T(8,128)(2,1)}) custom-call(bf16[128,3072]{1,0:T(8,128)(2,1)} %bitcast.7, bf16[128,3072]{1,0:T(8,128)(2,1)} %fresh.1, bf16[3072,2304]{1,0:T(8,128)(2,1)} %bitcast.5, bf16[3072,384]{1,0:T(8,128)(2,1)} %bitcast.6, bf16[128,3072]{1,0:T(8,128)(2,1)} %bitcast.8, f32[1,128]{1,0:T(1,128)} %q_gain_in.1, ...), custom_call_target="tpu_custom_call" | custom-call | flops 2000000000 | bytes 22000000 | tf_op jit(solution)/shard_map/relayed_block/pallas_call | solution.py:737
  68.9 27.9 %hand_over.1 = (bf16[128,3072]{1,0:T(8,128)(2,1)}, bf16[128,384]{1,0:T(8,128)(2,1)}) custom-call(bf16[128,3072]{1,0:T(8,128)(2,1)} %get-tuple-element.6.queue_in, bf16[128,384]{1,0:T(8,128)(2,1)} %get-tuple-element.7.clean_in), custom_call_target="tpu_custom_call" | custom-call | tf_op jit(solution)/shard_map/hand_over/pallas_call | solution.py:804

commit v3 on v2

--- a/solution.py
+++ b/solution.py
@@ -249,6 +249,7 @@
     own_att,
     att,
     done,
+    arrived,
     small_sem,
     local_sem,
     x_send,
@@ -265,6 +266,7 @@
     s_recv,
     c_send,
     c_recv,
+    out_sem,
 ):
     f = lax.axis_index("segment")
     q = lax.axis_index("seq")
@@ -292,6 +294,8 @@
             barrier, inc=1, device_id=(lax.rem(f + step, segments), q), device_id_type=MESH
         )
 
+    own_tokens = pltpu.make_async_copy(queue, tokens.at[0], local_sem.at[0])
+    own_tokens.start()
     small_loads = []
     for i, (source, target) in enumerate(
         ((rates_in, rates), (rope_in, rope), (q_gain_in, q_gain), (k_gain_in, k_gain))
@@ -299,8 +303,6 @@
         load = pltpu.make_async_copy(source, target, small_sem.at[i])
         load.start()
         small_loads.append(load)
-    own_tokens = pltpu.make_async_copy(queue, tokens.at[0], local_sem.at[0])
-    own_tokens.start()
     mod_depth = width // MOD_CHUNKS
     mod_loads = []
     for i in range(MOD_CHUNKS):
@@ -315,20 +317,22 @@
 
     pl.semaphore_wait(barrier, PEERS - 1 + segments - 1)
 
+    own_tokens.wait()
+
     piece = rows // X_CHUNKS
     mirror_x = []
     for i in range(X_CHUNKS):
         part = pl.ds(i * piece, piece)
         copy = remote(
-            queue.at[part], tokens.at[2, part], x_send.at[i], x_recv.at[i], (f, peers[2])
+            tokens.at[0, part], tokens.at[2, part], x_send.at[i], x_recv.at[i], (f, peers[2])
         )
         copy.start()
         mirror_x.append(copy)
     sibling_x = remote(
-        queue, tokens.at[1], x_send.at[X_CHUNKS], x_recv.at[X_CHUNKS], (f, peers[1])
+        tokens.at[0], tokens.at[1], x_send.at[X_CHUNKS], x_recv.at[X_CHUNKS], (f, peers[1])
     )
     sibling_x.start()
-    fresh_copy = pltpu.make_async_copy(fresh, queue_next, local_sem.at[3 + MOD_CHUNKS])
+    fresh_copy = pltpu.make_async_copy(fresh, arrived, local_sem.at[3 + MOD_CHUNKS])
 
     @pl.when(f == 0)
     def _():
@@ -412,7 +416,6 @@
     def modulate(x):
         return (x * mod_rows[:, width : 2 * width] + mod_rows[:, :width]).astype(jnp.bfloat16)
 
-    own_tokens.wait()
     forward_tokens(0)
     sibling_x.wait_recv()
     for rel in range(2):
@@ -651,7 +654,7 @@
         done[:, begin : begin + cols] = (kept + gate * projected).astype(jnp.bfloat16)
         shift = remote(
             done.at[:, part],
-            queue_next.at[:, part],
+            arrived.at[:, part],
             s_send.at[i],
             s_recv.at[i],
             (lax.rem(f + 1, segments), q),
@@ -690,15 +693,26 @@
     def _():
         fresh_copy.wait()
 
+    written = []
+    for i, shift in enumerate(shifts):
+
+        @pl.when(f > 0)
+        def _(shift=shift):
+            shift.wait_recv()
+
+        part = pl.ds(i * cols, cols)
+        copy = pltpu.make_async_copy(
+            arrived.at[:, part], queue_next.at[:, part], out_sem.at[i]
+        )
+        copy.start()
+        written.append(copy)
+    for copy in written:
+        copy.wait()
     for shift in shifts:
 
         @pl.when(f < last)
         def _(shift=shift):
             shift.wait_send()
-
-        @pl.when(f > 0)
-        def _(shift=shift):
-            shift.wait_recv()
 
     @pl.when(f == last)
     def _():
@@ -711,14 +725,25 @@
         cleans[0].wait_recv()
 
 
-def hand_over(queue_in, clean_in, queue_next, clean, sem):
-    copies = [
-        pltpu.make_async_copy(queue_in, queue_next, sem.at[0]),
-        pltpu.make_async_copy(clean_in, clean, sem.at[1]),
-    ]
-    for copy in copies:
+def hand_over(queue_in, clean_in, queue_next, clean, queue_held, clean_held, sem_in, sem_out):
+    piece = queue_in.shape[0] // X_CHUNKS
+    steps = []
+    for i in range(X_CHUNKS):
+        part = pl.ds(i * piece, piece)
+        steps.append((queue_in.at[part], queue_held.at[part], queue_next.at[part]))
+    steps.append((clean_in, clean_held, clean))
+    reads = []
+    for i, (source, held, _) in enumerate(steps):
+        copy = pltpu.make_async_copy(source, held, sem_in.at[i])
         copy.start()
-    for copy in copies:
+        reads.append(copy)
+    writes = []
+    for i, (_, held, target) in enumerate(steps):
+        reads[i].wait()
+        copy = pltpu.make_async_copy(held, target, sem_out.at[i])
+        copy.start()
+        writes.append(copy)
+    for copy in writes:
         copy.wait()
 
 
@@ -763,6 +788,7 @@
             pltpu.VMEM((PEERS, rows, head_dim), bf16),
             pltpu.VMEM((PEERS, rows, head_dim), bf16),
             pltpu.VMEM((rows, width), bf16),
+            pltpu.VMEM((rows, width), bf16),
             dma((4,)),
             dma((4 + MOD_CHUNKS,)),
             dma((2 * X_CHUNKS + 1,)),
@@ -779,6 +805,7 @@
             dma((OUT_CHUNKS,)),
             dma((segments,)),
             dma(()),
+            dma((OUT_CHUNKS,)),
         ],
         compiler_params=pltpu.CompilerParams(
             collective_id=0, has_side_effects=True, vmem_limit_bytes=56 * 1024 * 1024
@@ -809,7 +836,12 @@
         ),
         in_specs=[outside] * 2,
         out_specs=(outside, outside),
-        scratch_shapes=[dma((2,))],
+        scratch_shapes=[
+            pltpu.VMEM(queue_next.shape, bf16),
+            pltpu.VMEM(clean_frame.shape, bf16),
+            dma((X_CHUNKS + 1,)),
+            dma((X_CHUNKS + 1,)),
+        ],
         compiler_params=pltpu.CompilerParams(vmem_limit_bytes=56 * 1024 * 1024),
         name="hand_over",
     )(queue_next, clean_frame)

time: 97 us -> 71.6 us (0.74)
  Pallas kernels: 94.9 us -> 69.5 us
    pallas_call x1, Pallas kernels: 27.9 us -> 2.01 us  [fused(): pl.pallas_call(hand_over, out_shape=(jax.ShapeDtypeStruct(queue_next.shap...]
where the time goes in v3:
time: 71.6 us; the launch traced here: 71.4 us
  Pallas kernels  69.5 us (97%)
  between operations  1.93 us (3%)
    pallas_call x1, Pallas kernels, fused(): pl.pallas_call(functools.partial(block_kernel, segments, tuple(halves)),...  67.5 us
    pallas_call x1, Pallas kernels, fused(): pl.pallas_call(hand_over, out_shape=(jax.ShapeDtypeStruct(queue_next.shap...  2.01 us

profile of v3, /device:TPU:8, one launch (start us, length us, event | category | flops | bytes accessed | tf_op | source)
XLA Modules:
  0.0 71.4 jit_solution(9422144023966646239)
XLA Ops:
  1.9 67.5 %relayed_block.1 = (bf16[128,3072]{1,0:T(8,128)(2,1)}, bf16[128,384]{1,0:T(8,128)(2,1)}) custom-call(bf16[128,3072]{1,0:T(8,128)(2,1)} %bitcast.7, bf16[128,3072]{1,0:T(8,128)(2,1)} %fresh.1, bf16[3072,2304]{1,0:T(8,128)(2,1)} %bitcast.5, bf16[3072,384]{1,0:T(8,128)(2,1)} %bitcast.6, bf16[128,3072]{1,0:T(8,128)(2,1)} %bitcast.8, f32[1,128]{1,0:T(1,128)} %q_gain_in.1, ...), custom_call_target="tpu_custom_call" | custom-call | flops 2000000000 | bytes 22000000 | tf_op jit(solution)/shard_map/relayed_block/pallas_call | solution.py:762
  69.4 2.0 %hand_over.1 = (bf16[128,3072]{1,0:T(8,128)(2,1)}, bf16[128,384]{1,0:T(8,128)(2,1)}) custom-call(bf16[128,3072]{1,0:T(8,128)(2,1)} %get-tuple-element.6.queue_in, bf16[128,384]{1,0:T(8,128)(2,1)} %get-tuple-element.7.clean_in), custom_call_target="tpu_custom_call" | custom-call | tf_op jit(solution)/shard_map/hand_over/pallas_call | solution.py:831

commit v4 on v3

--- a/solution.py
+++ b/solution.py
@@ -246,6 +246,8 @@
     sines,
     queries,
     kv,
+    ranges,
+    mixes,
     own_att,
     att,
     done,
@@ -455,8 +457,8 @@
     halo = []
 
     def project(pieces, task):
-        count = len(pieces)
         at = sum(size for _, _, size in pieces)
+        base = (0, 2 * rows, 3 * rows)[task]
         joined = jnp.dot(normed[:at, :], qkv_w[...], preferred_element_type=jnp.float32)
         at = 0
         for rel, start, size in pieces:
@@ -474,26 +476,27 @@
                 return (x * cos + swapped * sin).astype(jnp.bfloat16)
 
             own = joined[at : at + size]
-            queries[rel, start : start + size, :] = turned(
+            queries[base + at : base + at + size, :] = turned(
                 own[:, :head_dim], q_gain[...] * score_scale
             )
-            kv[1, 0, rel, start : start + size, :] = turned(
+            kv[1, 0, base + at : base + at + size, :] = turned(
                 own[:, head_dim : 2 * head_dim], k_gain[...]
             )
-            kv[1, 1, rel, start : start + size, :] = own[:, 2 * head_dim :].astype(jnp.bfloat16)
+            kv[1, 1, base + at : base + at + size, :] = own[:, 2 * head_dim :].astype(
+                jnp.bfloat16
+            )
             at += size
-        rels = pl.ds(pieces[0][0], count)
-        part = pl.ds(pieces[0][1], pieces[0][2])
+        part = pl.ds(base, at)
         forth = remote(
-            kv.at[1, :, rels, part],
-            kv.at[0, :, rels, part],
+            kv.at[1, :, part],
+            kv.at[0, :, part],
             h_send.at[0, task],
             h_recv.at[0, task],
             (lax.rem(f + 1, segments), q),
         )
         back = remote(
-            kv.at[1, :, rels, part],
-            kv.at[2, :, rels, part],
+            kv.at[1, :, part],
+            kv.at[2, :, part],
             h_send.at[1, task],
             h_recv.at[1, task],
             (lax.rem(f + segments - 1, segments), q),
@@ -527,6 +530,82 @@
     sibling_w = remote(
         out_w.at[0], out_w.at[1], w_send.at[OUT_CHUNKS], w_recv.at[OUT_CHUNKS], (f, peers[1])
     )
+    counted = (
+        jnp.where(f > 0, 1.0, 0.0).astype(jnp.float32),
+        jnp.float32(1.0),
+        jnp.where(f < last, 1.0, 0.0).astype(jnp.float32),
+    )
+
+    def wait_halo(task):
+        forth, back = halo[task]
+        begin = (0, 2 * rows, 3 * rows)[task]
+        size = (2 * rows, rows, rows)[task]
+        part = slice(begin, begin + size)
+
+        @pl.when(f > 0)
+        def _():
+            forth.wait_recv()
+
+        @pl.when(f < last)
+        def _():
+            back.wait_recv()
+
+        for edge, side in ((0, 0), (last, 2)):
+
+            @pl.when(f == edge)
+            def _(side=side):
+                kv[side, 0, part, :] = kv[1, 0, part, :]
+                kv[side, 1, part, :] = jnp.zeros((size, head_dim), jnp.bfloat16)
+
+    def attend_to(block, begin, size):
+        own = queries[block * rows : (block + 1) * rows, :]
+        scores = [
+            lax.dot_general(
+                own,
+                kv[side, 0, begin : begin + size, :],
+                (((1,), (1,)), ((), ())),
+                preferred_element_type=jnp.float32,
+            )
+            for side in range(3)
+        ]
+        top = jnp.max(
+            jnp.maximum(jnp.maximum(scores[0], scores[2]), scores[1]), axis=1, keepdims=True
+        )
+        return scores, top
+
+    def mix(scores, top, begin, size):
+        weight = jnp.zeros((rows, 1), jnp.float32)
+        mixed = jnp.zeros((rows, head_dim), jnp.float32)
+        for side in range(3):
+            raised = jnp.exp2(scores[side] - top)
+            weight = weight + counted[side] * jnp.sum(raised, axis=1, keepdims=True)
+            mixed = mixed + jnp.dot(
+                raised.astype(jnp.bfloat16),
+                kv[side, 1, begin : begin + size, :],
+                preferred_element_type=jnp.float32,
+            )
+        return weight, mixed
+
+    early = 3 * rows
+
+    def attend_early(block):
+        part = slice(block * rows, (block + 1) * rows)
+        scores, top = attend_to(block, 0, early)
+        weight, mixed = mix(scores, top, 0, early)
+        ranges[0, part, :] = jnp.broadcast_to(top, (rows, head_dim))
+        ranges[1, part, :] = jnp.broadcast_to(weight, (rows, head_dim))
+        mixes[part, :] = mixed
+
+    def attend_late(block):
+        part = slice(block * rows, (block + 1) * rows)
+        scores, late_top = attend_to(block, early, rows)
+        early_top = ranges[0, part, :]
+        top = jnp.maximum(early_top, late_top)
+        weight, mixed = mix(scores, top[:, :1], early, rows)
+        keep = jnp.exp2(early_top - top)
+        weight = weight + ranges[1, part, :] * keep
+        return ((mixed + mixes[part, :] * keep) / weight).astype(jnp.bfloat16)
+
     project([(0, 0, rows), (1, 0, rows)], 0)
     half = rows // 2
     forward_tokens(2)
@@ -540,6 +619,9 @@
     norm_piece(2, half, piece, 0)
     forwards[2].wait_recv()
     norm_piece(3, half, piece, half)
+    wait_halo(0)
+    wait_halo(1)
+    attend_early(0)
     forward_tokens(3)
     send_weights(2)
     send_weights(3)
@@ -548,71 +630,23 @@
     norm_piece(3, half + piece, piece, half + piece)
     project([(2, half, half), (3, half, half)], 2)
     sibling_w.start()
-
-    @pl.when(f == 0)
-    def _():
-        kv[0, 0] = kv[1, 0]
-        kv[0, 1] = jnp.zeros_like(kv[0, 1])
-
-    @pl.when(f == last)
-    def _():
-        kv[2, 0] = kv[1, 0]
-        kv[2, 1] = jnp.zeros_like(kv[2, 1])
-
-    for forth, back in halo:
-
-        @pl.when(f > 0)
-        def _(forth=forth):
-            forth.wait_recv()
-
-        @pl.when(f < last)
-        def _(back=back):
-            back.wait_recv()
-
-    counted = (
-        jnp.where(f > 0, 1.0, 0.0).astype(jnp.float32),
-        jnp.float32(1.0),
-        jnp.where(f < last, 1.0, 0.0).astype(jnp.float32),
-    )
-    tokens_all = PEERS * rows
+    attend_early(1)
+    attend_early(2)
+    attend_early(3)
+    wait_halo(2)
     att_copies = []
-    for rel in (3, 2, 1, 0):
-        query_rows = queries[rel]
-        scores = []
-        for side in range(3):
-            key_rows = kv[side, 0].reshape(tokens_all, head_dim)
-            scores.append(
-                lax.dot_general(
-                    query_rows,
-                    key_rows,
-                    (((1,), (1,)), ((), ())),
-                    preferred_element_type=jnp.float32,
-                )
-            )
-        top = jnp.maximum(
-            jnp.max(jnp.maximum(scores[0], scores[2]), axis=1, keepdims=True),
-            jnp.max(scores[1], axis=1, keepdims=True),
-        )
-        weight = jnp.zeros((rows, 1), jnp.float32)
-        mixed = jnp.zeros((rows, head_dim), jnp.float32)
-        for side in range(3):
-            raised = jnp.exp2(scores[side] - top)
-            weight = weight + counted[side] * jnp.sum(raised, axis=1, keepdims=True)
-            mixed = mixed + jnp.dot(
-                raised.astype(jnp.bfloat16),
-                kv[side, 1].reshape(tokens_all, head_dim),
-                preferred_element_type=jnp.float32,
-            )
-        mixed = (mixed / weight).astype(jnp.bfloat16)
-        if rel == 0:
-            att[0] = mixed
+    both = [attend_late(2), attend_late(3)]
+    for rel in (3, 2, 1):
+        if rel == 1:
+            own_att[1] = attend_late(1)
         else:
-            own_att[rel] = mixed
-            copy = remote(
-                own_att.at[rel], att.at[rel], a_send.at[rel], a_recv.at[rel], (f, peers[rel])
-            )
-            copy.start()
-            att_copies.append(copy)
+            part = slice((rel - 2) * half, (rel - 1) * half)
+            own_att[rel, :half, :] = both[0][part]
+            own_att[rel, half:, :] = both[1][part]
+        copy = remote(own_att.at[rel], att.at[rel], a_send.at[rel], a_recv.at[rel], (f, peers[rel]))
+        copy.start()
+        att_copies.append(copy)
+    att[0] = attend_late(0)
 
     forward_w = []
 
@@ -783,8 +817,10 @@
             pltpu.VMEM((2 * rows, width), bf16),
             pltpu.VMEM((PEERS, rows, head_dim), f32),
             pltpu.VMEM((PEERS, rows, head_dim), f32),
-            pltpu.VMEM((PEERS, rows, head_dim), bf16),
-            pltpu.VMEM((3, 2, PEERS, rows, head_dim), bf16),
+            pltpu.VMEM((PEERS * rows, head_dim), bf16),
+            pltpu.VMEM((3, 2, PEERS * rows, head_dim), bf16),
+            pltpu.VMEM((2, PEERS * rows, head_dim), f32),
+            pltpu.VMEM((PEERS * rows, head_dim), f32),
             pltpu.VMEM((PEERS, rows, head_dim), bf16),
             pltpu.VMEM((PEERS, rows, head_dim), bf16),
             pltpu.VMEM((rows, width), bf16),

time: 71.6 us -> 74.4 us (1.039)
  Pallas kernels: 69.5 us -> 72.3 us
    pallas_call x1, Pallas kernels: 67.5 us -> 70.3 us  [fused(): pl.pallas_call(functools.partial(block_kernel, segments, tuple(halves)),...]
where the time goes in v4:
time: 74.4 us; the launch traced here: 74.3 us
  Pallas kernels  72.3 us (97%)
  between operations  1.93 us (3%)
    pallas_call x1, Pallas kernels, fused(): pl.pallas_call(functools.partial(block_kernel, segments, tuple(halves)),...  70.3 us
    pallas_call x1, Pallas kernels, fused(): pl.pallas_call(hand_over, out_shape=(jax.ShapeDtypeStruct(queue_next.shap...  2.01 us

profile of v4, /device:TPU:8, one launch (start us, length us, event | category | flops | bytes accessed | tf_op | source)
XLA Modules:
  0.0 74.3 jit_solution(17348460761096344367)
XLA Ops:
  1.9 70.3 %relayed_block.1 = (bf16[128,3072]{1,0:T(8,128)(2,1)}, bf16[128,384]{1,0:T(8,128)(2,1)}) custom-call(bf16[128,3072]{1,0:T(8,128)(2,1)} %bitcast.7, bf16[128,3072]{1,0:T(8,128)(2,1)} %fresh.1, bf16[3072,2304]{1,0:T(8,128)(2,1)} %bitcast.5, bf16[3072,384]{1,0:T(8,128)(2,1)} %bitcast.6, bf16[128,3072]{1,0:T(8,128)(2,1)} %bitcast.8, f32[1,128]{1,0:T(1,128)} %q_gain_in.1, ...), custom_call_target="tpu_custom_call" | custom-call | flops 2000000000 | bytes 22000000 | tf_op jit(solution)/shard_map/relayed_block/pallas_call | solution.py:796
  72.3 2.0 %hand_over.1 = (bf16[128,3072]{1,0:T(8,128)(2,1)}, bf16[128,384]{1,0:T(8,128)(2,1)}) custom-call(bf16[128,3072]{1,0:T(8,128)(2,1)} %get-tuple-element.6.queue_in, bf16[128,384]{1,0:T(8,128)(2,1)} %get-tuple-element.7.clean_in), custom_call_target="tpu_custom_call" | custom-call | tf_op jit(solution)/shard_map/hand_over/pallas_call | solution.py:867

commit v5 on v4

--- a/solution.py
+++ b/solution.py
@@ -240,7 +240,7 @@
     q_gain,
     k_gain,
     embedded,
-    settled,
+    kept,
     normed,
     cosines,
     sines,
@@ -296,7 +296,7 @@
             barrier, inc=1, device_id=(lax.rem(f + step, segments), q), device_id_type=MESH
         )
 
-    own_tokens = pltpu.make_async_copy(queue, tokens.at[0], local_sem.at[0])
+    own_tokens = pltpu.make_async_copy(queue, kept, local_sem.at[0])
     own_tokens.start()
     small_loads = []
     for i, (source, target) in enumerate(
@@ -321,9 +321,18 @@
 
     own_tokens.wait()
 
+    def settle_rows(i, carry):
+        offset = pl.multiple_of(i * 16, 16)
+        x = kept[pl.ds(offset, 16), :].astype(jnp.float32)
+        x = x - jnp.mean(x, axis=1, keepdims=True)
+        x = x * lax.rsqrt(jnp.mean(x * x, axis=1, keepdims=True) + EPSILON)
+        tokens[0, pl.ds(offset, 16), :] = x.astype(jnp.bfloat16)
+        return carry
+
     piece = rows // X_CHUNKS
     mirror_x = []
     for i in range(X_CHUNKS):
+        lax.fori_loop(i * piece // 16, (i + 1) * piece // 16, settle_rows, 0, unroll=True)
         part = pl.ds(i * piece, piece)
         copy = remote(
             tokens.at[0, part], tokens.at[2, part], x_send.at[i], x_recv.at[i], (f, peers[2])
@@ -410,49 +419,31 @@
         copy.start()
         forwards.append(copy)
 
-    def settle(x):
-        x = x.astype(jnp.float32)
-        x = x - jnp.mean(x, axis=1, keepdims=True)
-        return x * lax.rsqrt(jnp.mean(x * x, axis=1, keepdims=True) + EPSILON)
-
-    def modulate(x):
-        return (x * mod_rows[:, width : 2 * width] + mod_rows[:, :width]).astype(jnp.bfloat16)
-
     forward_tokens(0)
     sibling_x.wait_recv()
-    for rel in range(2):
-
-        def settle_rows(i, carry, rel=rel):
-            offset = pl.multiple_of(i * 16, 16)
-            settled[pl.ds(rel * rows + offset, 16), :] = settle(tokens[rel, pl.ds(offset, 16), :])
-            return carry
-
-        lax.fori_loop(0, rows // 16, settle_rows, 0, unroll=4)
     forward_tokens(1)
     qkv_load.wait()
     out_load.wait()
     for copy in mod_copies:
         copy.wait()
     for peer in range(PEERS):
-        mod_rows[:, peer * mod_cols : (peer + 1) * mod_cols] = mod_all[peer]
+        mod_rows[:, peer * mod_cols : (peer + 1) * mod_cols] = jnp.broadcast_to(
+            mod_all[peer], (8, mod_cols)
+        )
     mod_rows[:, width : 2 * width] = 1.0 + mod_rows[:, width : 2 * width]
-
-    def modulate_rows(i, carry):
-        offset = pl.multiple_of(i * 16, 16)
-        normed[pl.ds(offset, 16), :] = modulate(settled[pl.ds(offset, 16), :])
-        return carry
-
-    lax.fori_loop(0, 2 * rows // 16, modulate_rows, 0, unroll=4)
 
     def norm_piece(rel, start, size, at):
         def norm_rows(i, carry):
             offset = pl.multiple_of(i * 16, 16)
-            x = settle(tokens[rel, pl.ds(start + offset, 16), :])
-            normed[pl.ds(at + offset, 16), :] = modulate(x)
+            x = tokens[rel, pl.ds(start + offset, 16), :].astype(jnp.float32)
+            x = x.reshape(2, 8, width) * mod_rows[:, width : 2 * width] + mod_rows[:, :width]
+            normed[pl.ds(at + offset, 16), :] = x.reshape(16, width).astype(jnp.bfloat16)
             return carry
 
-        lax.fori_loop(0, size // 16, norm_rows, 0, unroll=True)
-
+        lax.fori_loop(0, size // 16, norm_rows, 0, unroll=2)
+
+    norm_piece(0, 0, rows, 0)
+    norm_piece(1, 0, rows, rows)
     score_scale = head_dim ** (-0.5) * math.log2(math.e)
     halo = []
 
@@ -619,9 +610,6 @@
     norm_piece(2, half, piece, 0)
     forwards[2].wait_recv()
     norm_piece(3, half, piece, half)
-    wait_halo(0)
-    wait_halo(1)
-    attend_early(0)
     forward_tokens(3)
     send_weights(2)
     send_weights(3)
@@ -630,9 +618,10 @@
     norm_piece(3, half + piece, piece, half + piece)
     project([(2, half, half), (3, half, half)], 2)
     sibling_w.start()
-    attend_early(1)
-    attend_early(2)
-    attend_early(3)
+    wait_halo(0)
+    wait_halo(1)
+    for block in range(PEERS):
+        attend_early(block)
     wait_halo(2)
     att_copies = []
     both = [attend_late(2), attend_late(3)]
@@ -684,8 +673,9 @@
             preferred_element_type=jnp.float32,
         )
         gate = mod_rows[:, 2 * width + begin : 2 * width + begin + cols]
-        kept = tokens[0, :, begin : begin + cols].astype(jnp.float32)
-        done[:, begin : begin + cols] = (kept + gate * projected).astype(jnp.bfloat16)
+        gated = (projected.reshape(rows // 8, 8, cols) * gate).reshape(rows, cols)
+        before = kept[:, begin : begin + cols].astype(jnp.float32)
+        done[:, begin : begin + cols] = (before + gated).astype(jnp.bfloat16)
         shift = remote(
             done.at[:, part],
             arrived.at[:, part],
@@ -807,13 +797,13 @@
             pltpu.VMEM((PEERS, rows, width), bf16),
             pltpu.VMEM((PEERS, rows, width), bf16),
             pltpu.VMEM((PEERS, 1, mod_cols), f32),
-            pltpu.VMEM((1, 3 * width), f32),
+            pltpu.VMEM((8, 3 * width), f32),
             pltpu.VMEM((1, width // 2), f32),
             pltpu.VMEM((8, head_dim), f32),
             pltpu.VMEM((1, head_dim), f32),
             pltpu.VMEM((1, head_dim), f32),
             pltpu.VMEM((width, LANES), f32),
-            pltpu.VMEM((2 * rows, width), f32),
+            pltpu.VMEM((rows, width), bf16),
             pltpu.VMEM((2 * rows, width), bf16),
             pltpu.VMEM((PEERS, rows, head_dim), f32),
             pltpu.VMEM((PEERS, rows, head_dim), f32),

time: 74.4 us -> 71.9 us (0.966)
  Pallas kernels: 72.3 us -> 69.8 us
    pallas_call x1, Pallas kernels: 70.3 us -> 67.8 us  [fused(): pl.pallas_call(functools.partial(block_kernel, segments, tuple(halves)),...]
where the time goes in v5:
time: 71.9 us; the launch traced here: 71.8 us
  Pallas kernels  69.8 us (97%)
  between operations  1.93 us (3%)
    pallas_call x1, Pallas kernels, fused(): pl.pallas_call(functools.partial(block_kernel, segments, tuple(halves)),...  67.8 us
    pallas_call x1, Pallas kernels, fused(): pl.pallas_call(hand_over, out_shape=(jax.ShapeDtypeStruct(queue_next.shap...  2.01 us

profile of v5, /device:TPU:8, one launch (start us, length us, event | category | flops | bytes accessed | tf_op | source)
XLA Modules:
  0.0 71.8 jit_solution(2163801271185809928)
XLA Ops:
  1.9 67.8 %relayed_block.1 = (bf16[128,3072]{1,0:T(8,128)(2,1)}, bf16[128,384]{1,0:T(8,128)(2,1)}) custom-call(bf16[128,3072]{1,0:T(8,128)(2,1)} %bitcast.7, bf16[128,3072]{1,0:T(8,128)(2,1)} %fresh.1, bf16[3072,2304]{1,0:T(8,128)(2,1)} %bitcast.5, bf16[3072,384]{1,0:T(8,128)(2,1)} %bitcast.6, bf16[128,3072]{1,0:T(8,128)(2,1)} %bitcast.8, f32[1,128]{1,0:T(1,128)} %q_gain_in.1, ...), custom_call_target="tpu_custom_call" | custom-call | flops 2000000000 | bytes 22000000 | tf_op jit(solution)/shard_map/relayed_block/pallas_call | solution.py:786
  69.7 2.0 %hand_over.1 = (bf16[128,3072]{1,0:T(8,128)(2,1)}, bf16[128,384]{1,0:T(8,128)(2,1)}) custom-call(bf16[128,3072]{1,0:T(8,128)(2,1)} %get-tuple-element.6.queue_in, bf16[128,384]{1,0:T(8,128)(2,1)} %get-tuple-element.7.clean_in), custom_call_target="tpu_custom_call" | custom-call | tf_op jit(solution)/shard_map/hand_over/pallas_call | solution.py:857

commit v6 on v5

--- a/solution.py
+++ b/solution.py
@@ -182,7 +182,7 @@
 PEERS = 4
 MOD_CHUNKS = 6
 X_CHUNKS = 4
-OUT_CHUNKS = 4
+OUT_CHUNKS = 8
 LANES = 128
 
 
@@ -607,21 +607,23 @@
         norm_piece(3, i * piece, piece, half + i * piece)
     project([(2, 0, half), (3, 0, half)], 1)
     send_weights(1)
+    send_weights(2)
     norm_piece(2, half, piece, 0)
     forwards[2].wait_recv()
     norm_piece(3, half, piece, half)
     forward_tokens(3)
-    send_weights(2)
     send_weights(3)
     norm_piece(2, half + piece, piece, piece)
     forwards[3].wait_recv()
     norm_piece(3, half + piece, piece, half + piece)
     project([(2, half, half), (3, half, half)], 2)
+    send_weights(4)
     sibling_w.start()
     wait_halo(0)
     wait_halo(1)
     for block in range(PEERS):
         attend_early(block)
+    send_weights(5)
     wait_halo(2)
     att_copies = []
     both = [attend_late(2), attend_late(3)]
@@ -635,6 +637,8 @@
         copy = remote(own_att.at[rel], att.at[rel], a_send.at[rel], a_recv.at[rel], (f, peers[rel]))
         copy.start()
         att_copies.append(copy)
+    for i in range(6, OUT_CHUNKS):
+        send_weights(i)
     att[0] = attend_late(0)
 
     forward_w = []

time: 71.9 us -> 72 us (level)
  no operation moved by 1% of the time
where the time goes in v6:
time: 72 us; the launch traced here: 71.8 us
  Pallas kernels  69.9 us (97%)
  between operations  1.93 us (3%)
    pallas_call x1, Pallas kernels, fused(): pl.pallas_call(functools.partial(block_kernel, segments, tuple(halves)),...  67.8 us
    pallas_call x1, Pallas kernels, fused(): pl.pallas_call(hand_over, out_shape=(jax.ShapeDtypeStruct(queue_next.shap...  2.01 us

profile of v6, /device:TPU:8, one launch (start us, length us, event | category | flops | bytes accessed | tf_op | source)
XLA Modules:
  0.0 71.8 jit_solution(6788530727637974812)
XLA Ops:
  1.9 67.8 %relayed_block.1 = (bf16[128,3072]{1,0:T(8,128)(2,1)}, bf16[128,384]{1,0:T(8,128)(2,1)}) custom-call(bf16[128,3072]{1,0:T(8,128)(2,1)} %bitcast.7, bf16[128,3072]{1,0:T(8,128)(2,1)} %fresh.1, bf16[3072,2304]{1,0:T(8,128)(2,1)} %bitcast.5, bf16[3072,384]{1,0:T(8,128)(2,1)} %bitcast.6, bf16[128,3072]{1,0:T(8,128)(2,1)} %bitcast.8, f32[1,128]{1,0:T(1,128)} %q_gain_in.1, ...), custom_call_target="tpu_custom_call" | custom-call | flops 2000000000 | bytes 22000000 | tf_op jit(solution)/shard_map/relayed_block/pallas_call | solution.py:790
  69.8 2.0 %hand_over.1 = (bf16[128,3072]{1,0:T(8,128)(2,1)}, bf16[128,384]{1,0:T(8,128)(2,1)}) custom-call(bf16[128,3072]{1,0:T(8,128)(2,1)} %get-tuple-element.6.queue_in, bf16[128,384]{1,0:T(8,128)(2,1)} %get-tuple-element.7.clean_in), custom_call_target="tpu_custom_call" | custom-call | tf_op jit(solution)/shard_map/hand_over/pallas_call | solution.py:861

commit v7 on v6

--- a/solution.py
+++ b/solution.py
@@ -600,19 +600,17 @@
     project([(0, 0, rows), (1, 0, rows)], 0)
     half = rows // 2
     forward_tokens(2)
-    send_weights(0)
     for i in range(2):
         forwards[i].wait_recv()
         norm_piece(2, i * piece, piece, i * piece)
         norm_piece(3, i * piece, piece, half + i * piece)
     project([(2, 0, half), (3, 0, half)], 1)
-    send_weights(1)
-    send_weights(2)
     norm_piece(2, half, piece, 0)
     forwards[2].wait_recv()
     norm_piece(3, half, piece, half)
     forward_tokens(3)
-    send_weights(3)
+    for i in range(4):
+        send_weights(i)
     norm_piece(2, half + piece, piece, piece)
     forwards[3].wait_recv()
     norm_piece(3, half + piece, piece, half + piece)

time: 72 us -> 72.2 us (level)
  no operation moved by 1% of the time
where the time goes in v7:
time: 72.2 us; the launch traced here: 72 us
  Pallas kernels  70 us (97%)
  between operations  1.93 us (3%)
    pallas_call x1, Pallas kernels, fused(): pl.pallas_call(functools.partial(block_kernel, segments, tuple(halves)),...  68 us
    pallas_call x1, Pallas kernels, fused(): pl.pallas_call(hand_over, out_shape=(jax.ShapeDtypeStruct(queue_next.shap...  2.01 us

profile of v7, /device:TPU:8, one launch (start us, length us, event | category | flops | bytes accessed | tf_op | source)
XLA Modules:
  0.0 72.0 jit_solution(13682662473632390222)
XLA Ops:
  1.9 68.0 %relayed_block.1 = (bf16[128,3072]{1,0:T(8,128)(2,1)}, bf16[128,384]{1,0:T(8,128)(2,1)}) custom-call(bf16[128,3072]{1,0:T(8,128)(2,1)} %bitcast.7, bf16[128,3072]{1,0:T(8,128)(2,1)} %fresh.1, bf16[3072,2304]{1,0:T(8,128)(2,1)} %bitcast.5, bf16[3072,384]{1,0:T(8,128)(2,1)} %bitcast.6, bf16[128,3072]{1,0:T(8,128)(2,1)} %bitcast.8, f32[1,128]{1,0:T(1,128)} %q_gain_in.1, ...), custom_call_target="tpu_custom_call" | custom-call | flops 2000000000 | bytes 22000000 | tf_op jit(solution)/shard_map/relayed_block/pallas_call | solution.py:788
  70.0 2.0 %hand_over.1 = (bf16[128,3072]{1,0:T(8,128)(2,1)}, bf16[128,384]{1,0:T(8,128)(2,1)}) custom-call(bf16[128,3072]{1,0:T(8,128)(2,1)} %get-tuple-element.6.queue_in, bf16[128,384]{1,0:T(8,128)(2,1)} %get-tuple-element.7.clean_in), custom_call_target="tpu_custom_call" | custom-call | tf_op jit(solution)/shard_map/hand_over/pallas_call | solution.py:859
